TPU v7x, 32 devices: a whole 2x2x4 slice. The times are simulated.
32 devices in a mesh: seq: 4 (over y, x), mp: 8 (over z, core).
Axes of the slice: x: 2, y: 2, z: 4, core: 2. Of those that a mesh axis runs over, the one named last changes fastest.
Arguments:
- features: bfloat16 [8192, 16384], P('seq', 'mp'), may hold values from -6 to 6
- coupling: bfloat16 [8192, 256], P('seq'), may hold values from -6 to 6
- gate_values: bfloat16 [8192, 16384], P('seq', 'mp'), may hold values from -40 to 40
- step_raw: float32 [256, 8192], P('mp', 'seq'), may hold values from -12 to 8192
- decay_log: float32 [256], P('mp'), may hold values from -8 to 0
- feature_taps: float32 [4, 16384], P(None, 'mp'), may hold values from -3 to 3
- feature_offset: float32 [16384], P('mp'), may hold values from -3 to 3
- coupling_taps: float32 [4, 256], replicated, may hold values from -3 to 3
- coupling_offset: float32 [256], replicated, may hold values from -3 to 3
- norm_gain: float32 [16384], P('mp'), may hold values from 0.25 to 1.75
Outputs:
- normalized: bfloat16 [8192, 16384], P('seq', 'mp')
All inputs are finite; a program needn't handle non-finite values.
Results may differ from a plain program's by a relative error of at most 0.0061.
Values may be sent and summed in bfloat16 or wider, within the bound.
A program may use at most 128 MiB of HBM per device.

v0:
```python
import jax
import jax.numpy as jnp
from jax import lax
from jax.sharding import PartitionSpec as P

BLOCK = 256
INNER = 16384


FULL_PRECISION = lax.Precision.HIGHEST


def passed_along(block, axis, distance):
    devices = range(lax.axis_size(axis))
    route = [(i - distance, i) for i in devices if i - distance in devices]
    return lax.ppermute(block, axis, route)


def causal_mix(previous, current, weight, bias_row):
    tap_count = weight.shape[0]
    length = current.shape[0]
    padded = jnp.concatenate([previous, current], axis=0)
    running = jnp.zeros(current.shape, jnp.float32) + bias_row[None, :]
    for offset in range(tap_count):
        running = running + weight[offset][None, :] * padded[offset : offset + length].astype(
            jnp.float32
        )
    return jax.nn.silu(running).astype(jnp.bfloat16)


def block_pass(state_now, inputs):
    feature_block, input_map, output_map, step_block, log_block = inputs
    head_count, block_len = step_block.shape
    feature = feature_block.shape[1] // head_count
    per_head = feature_block.astype(jnp.float32).reshape(block_len, head_count, feature)
    scores = jnp.dot(output_map, input_map.T, precision=FULL_PRECISION)
    spread = log_block[:, :, None] - log_block[:, None, :]
    causal = (jnp.arange(block_len)[:, None] >= jnp.arange(block_len)[None, :])[None, :, :]
    weights = jnp.where(causal, jnp.exp(jnp.where(causal, spread, 0.0)), 0.0)
    weights = weights * scores[None, :, :] * step_block[:, None, :]
    inside = jnp.einsum("hts,shp->thp", weights, per_head, precision=FULL_PRECISION)
    carried = jnp.einsum("tn,hpn->thp", output_map, state_now, precision=FULL_PRECISION)
    carried = carried * jnp.exp(log_block).T[:, :, None]
    ending = log_block[:, -1]
    to_end = jnp.exp(ending[:, None] - log_block) * step_block
    weighted = per_head * to_end.T[:, :, None]
    fresh_part = jnp.einsum("shp,sn->hpn", weighted, input_map, precision=FULL_PRECISION)
    new_state = jnp.exp(ending)[:, None, None] * state_now + fresh_part
    return (new_state, (inside + carried).reshape(block_len, head_count * feature))


def on_device(
    features,
    coupling,
    gate_values,
    step_raw,
    decay_log,
    feature_taps,
    feature_offset,
    coupling_taps,
    coupling_offset,
    norm_gain,
):
    tok_count = features.shape[0]
    tap_count = feature_taps.shape[0]
    head_count = decay_log.shape[0]
    state_size = coupling.shape[1] // 2
    feature = features.shape[1] // head_count
    tail_start = tok_count - tap_count + 1
    prior_features, prior_coupling = passed_along(
        (features[tail_start:], coupling[tail_start:]), "seq", 1
    )
    filtered = causal_mix(prior_features, features, feature_taps, feature_offset)
    coupled = causal_mix(prior_coupling, coupling, coupling_taps, coupling_offset).astype(
        jnp.float32
    )
    input_map = coupled[:, :state_size]
    output_map = coupled[:, state_size:]
    increment_amount = jax.nn.softplus(step_raw)
    log_decay = -jnp.exp(decay_log)[:, None] * increment_amount
    blocks = tok_count // BLOCK
    log_inside = jnp.cumsum(log_decay.reshape(head_count, blocks, BLOCK), axis=2)
    inputs = (
        filtered.reshape(blocks, BLOCK, head_count * feature),
        input_map.reshape(blocks, BLOCK, state_size),
        output_map.reshape(blocks, BLOCK, state_size),
        increment_amount.reshape(head_count, blocks, BLOCK).transpose(1, 0, 2),
        log_inside.transpose(1, 0, 2),
    )
    zero_state = jnp.zeros((head_count, feature, state_size), jnp.float32)
    local_end, local_out = lax.scan(block_pass, zero_state, inputs)
    local_out = local_out.reshape(tok_count, head_count * feature)
    section_decay = jnp.exp(jnp.sum(log_decay, axis=1))

    def relay_step(turn_index, incoming):
        return passed_along(section_decay[:, None, None] * incoming + local_end, "seq", 1)

    entering = lax.fori_loop(0, lax.axis_size("seq") - 1, relay_step, jnp.zeros_like(local_end))
    log_running = jnp.cumsum(log_decay, axis=1)
    from_before = jnp.einsum("tn,hpn->thp", output_map, entering, precision=FULL_PRECISION)
    from_before = from_before * jnp.exp(log_running).T[:, :, None]
    scan_values = local_out + from_before.reshape(tok_count, head_count * feature)
    gated_values = scan_values * jax.nn.silu(gate_values.astype(jnp.float32))
    squares = lax.psum(jnp.sum(gated_values * gated_values, axis=1), "mp")
    mean_square = squares / INNER
    return (gated_values * norm_gain[None, :] * lax.rsqrt(mean_square + 1e-05)[:, None]).astype(
        jnp.bfloat16
    )


def solution(mesh):
    in_specs = (
        P("seq", "mp"),
        P("seq", None),
        P("seq", "mp"),
        P("mp", "seq"),
        P("mp"),
        P(None, "mp"),
        P("mp"),
        P(),
        P(),
        P("mp"),
    )
    out_specs = P("seq", "mp")
    return jax.shard_map(
        on_device, mesh=mesh, in_specs=in_specs, out_specs=out_specs, check_vma=False
    )
```

profile of v0, /device:TPU:0, one launch (start us, length us, event | category | flops | bytes accessed | tf_op | source)
XLA Modules:
  0.0 417.6 jit_solution(10723577797781792679)
XLA Ops:
  0.8 4.8 %collective-permute-start.2 = (bf16[3,256]{1,0:T(4,128)(2,1)S(1)}, bf16[3,256]{1,0:T(4,128)(2,1)S(1)}, u32[]{:S(2)}, u32[]{:S(2)}) collective-permute-start(bf16[3,256]{1,0:T(4,128)(2,1)S(1)} %slice.82), channel_id=1, source_target_pairs={{0,8},{8,16},{16,24},{1,9},{9,17},{17,25},{2,10},{10,18},{18,26},{... | collective-permute-start | bytes 4616 | tf_op jit(solution)/shard_map/ppermute | solution.py:16
  6.4 3.4 collective-permute-start.1
  12.9 9.1 %reduce-window.16 = f32[32,16,128]{2,1,0:T(8,128)S(1)} reduce-window(f32[32,16,128]{2,1,0:T(8,128)S(1)} %bitcast.124, f32[]{:T(128)} %constant.42.clone.1), window={size=1x1x128 pad=0_0x0_0x127_0}, to_apply=%region_7.8 | reduce-window | flops 8323072 | bytes 524292 | tf_op jit(solution)/shard_map/reduce-window.2
  22.8 18.0 %reduce-window.14 = f32[32,8,2,128]{3,1,2,0:T(8,128)S(1)} reduce-window(f32[32,8,2,128]{3,1,2,0:T(8,128)S(1)} %copy.26, f32[]{:T(128)} %constant.42.clone.1), window={size=1x1x1x128 pad=0_0x0_0x0_0x127_0}, to_apply=%region_0.1 | reduce-window | flops 8323072 | bytes 524292 | tf_op jit(solution)/shard_map/reduce-window
  45.1 2.2 multiply_convert_fusion.2
  49.8 19.4 %multiply_convert_fusion.1 = bf16[2048,2048]{1,0:T(8,128)(2,1)} fusion(bf16[2048,2048]{1,0:T(8,128)(2,1)} %param.14, bf16[3,2048]{1,0:T(4,128)(2,1)S(1)} %collective-permute-done.1, f32[2048]{0:T(1024)S(1)} %bitcast.131, f32[2048]{0:T(1024)S(1)} %bitcast.132, f32[2048]{0:T(1024)S(1)} %bitcast.130, f32[2048]{0:T(1024)S(1)} %bitcast.129, f32[2048]{0:T(1024)S(1)} %copy-done.3), kind=kLoop, calls=%fused_computation.54 | loop fusion | flops 109051904 | bytes 16830464 | tf_op jit(solution)/shard_map/convert_element_type | solution.py:28
  69.2 200.2 %while.24 = (s32[]{:T(128)}, f32[32,64,128]{2,1,0:T(8,128)S(1)}, f32[8,256,2048]{2,1,0:T(8,128)}, f32[8,32,256]{2,0,1:T(8,128)}, bf16[8,256,2048]{2,1,0:T(8,128)...) while((s32[]{:T(128)}, f32[32,64,128]{2,1,0:T(8,128)S(1)}, ...), condition=%wide.region_3.4_spmd.clone, body=%wide.region_2.3_spmd.clone.sunk | while | flops 3335602176 | bytes 30181264 | solution.py:91
  76.1 2.7 fusion.72
  78.9 8.9 %bitcast_add_fusion.3 = f32[256,32,64]{0,2,1:T(8,128)} fusion(f32[256,32,64]{0,2,1:T(8,128)S(1)} %fusion.72, bf16[256,32,64]{0,2,1:T(8,128)(2,1)S(1)} %bitcast.116, f32[32,256]{1,0:T(8,128)S(1)} %copy.64, f32[256,256]{1,0:T(8,128)S(1)} %fusion.73, f32[32,256]{1,0:T(8,128)} %bitcast.126, pred[256,256]{1,0:T(8,128)(4,1)S(1)} %iota_compare_fusion.2, ...), kind=kOutput, calls=%fused_computation.14.clone.1 | convolution fusion | flops 1622147072 | bytes 5668864 | tf_op jit(solution)/shard_map/while/body/eval_jaxpr/hts,shp->thp/dot_general | solution.py:41
  87.7 3.1 convolution_add_fusion.2
  90.8 1.9 copy.67
  101.1 2.7 fusion.72
  103.9 8.9 %bitcast_add_fusion.3 = f32[256,32,64]{0,2,1:T(8,128)} fusion(f32[256,32,64]{0,2,1:T(8,128)S(1)} %fusion.72, bf16[256,32,64]{0,2,1:T(8,128)(2,1)S(1)} %bitcast.116, f32[32,256]{1,0:T(8,128)S(1)} %copy.64, f32[256,256]{1,0:T(8,128)S(1)} %fusion.73, f32[32,256]{1,0:T(8,128)} %bitcast.126, pred[256,256]{1,0:T(8,128)(4,1)S(1)} %iota_compare_fusion.2, ...), kind=kOutput, calls=%fused_computation.14.clone.1 | convolution fusion | flops 1622147072 | bytes 5668864 | tf_op jit(solution)/shard_map/while/body/eval_jaxpr/hts,shp->thp/dot_general | solution.py:41
  112.7 3.1 convolution_add_fusion.2
  115.9 1.9 copy.67
  126.1 2.7 fusion.72
  128.9 8.9 %bitcast_add_fusion.3 = f32[256,32,64]{0,2,1:T(8,128)} fusion(f32[256,32,64]{0,2,1:T(8,128)S(1)} %fusion.72, bf16[256,32,64]{0,2,1:T(8,128)(2,1)S(1)} %bitcast.116, f32[32,256]{1,0:T(8,128)S(1)} %copy.64, f32[256,256]{1,0:T(8,128)S(1)} %fusion.73, f32[32,256]{1,0:T(8,128)} %bitcast.126, pred[256,256]{1,0:T(8,128)(4,1)S(1)} %iota_compare_fusion.2, ...), kind=kOutput, calls=%fused_computation.14.clone.1 | convolution fusion | flops 1622147072 | bytes 5668864 | tf_op jit(solution)/shard_map/while/body/eval_jaxpr/hts,shp->thp/dot_general | solution.py:41
  137.7 3.1 convolution_add_fusion.2
  140.9 1.9 copy.67
  151.1 2.7 fusion.72
  153.9 8.9 %bitcast_add_fusion.3 = f32[256,32,64]{0,2,1:T(8,128)} fusion(f32[256,32,64]{0,2,1:T(8,128)S(1)} %fusion.72, bf16[256,32,64]{0,2,1:T(8,128)(2,1)S(1)} %bitcast.116, f32[32,256]{1,0:T(8,128)S(1)} %copy.64, f32[256,256]{1,0:T(8,128)S(1)} %fusion.73, f32[32,256]{1,0:T(8,128)} %bitcast.126, pred[256,256]{1,0:T(8,128)(4,1)S(1)} %iota_compare_fusion.2, ...), kind=kOutput, calls=%fused_computation.14.clone.1 | convolution fusion | flops 1622147072 | bytes 5668864 | tf_op jit(solution)/shard_map/while/body/eval_jaxpr/hts,shp->thp/dot_general | solution.py:41
  162.7 3.1 convolution_add_fusion.2
  176.2 2.7 fusion.72
  178.9 8.9 %bitcast_add_fusion.3 = f32[256,32,64]{0,2,1:T(8,128)} fusion(f32[256,32,64]{0,2,1:T(8,128)S(1)} %fusion.72, bf16[256,32,64]{0,2,1:T(8,128)(2,1)S(1)} %bitcast.116, f32[32,256]{1,0:T(8,128)S(1)} %copy.64, f32[256,256]{1,0:T(8,128)S(1)} %fusion.73, f32[32,256]{1,0:T(8,128)} %bitcast.126, pred[256,256]{1,0:T(8,128)(4,1)S(1)} %iota_compare_fusion.2, ...), kind=kOutput, calls=%fused_computation.14.clone.1 | convolution fusion | flops 1622147072 | bytes 5668864 | tf_op jit(solution)/shard_map/while/body/eval_jaxpr/hts,shp->thp/dot_general | solution.py:41
  187.8 3.1 convolution_add_fusion.2
  201.3 2.7 fusion.72
  204.0 8.9 %bitcast_add_fusion.3 = f32[256,32,64]{0,2,1:T(8,128)} fusion(f32[256,32,64]{0,2,1:T(8,128)S(1)} %fusion.72, bf16[256,32,64]{0,2,1:T(8,128)(2,1)S(1)} %bitcast.116, f32[32,256]{1,0:T(8,128)S(1)} %copy.64, f32[256,256]{1,0:T(8,128)S(1)} %fusion.73, f32[32,256]{1,0:T(8,128)} %bitcast.126, pred[256,256]{1,0:T(8,128)(4,1)S(1)} %iota_compare_fusion.2, ...), kind=kOutput, calls=%fused_computation.14.clone.1 | convolution fusion | flops 1622147072 | bytes 5668864 | tf_op jit(solution)/shard_map/while/body/eval_jaxpr/hts,shp->thp/dot_general | solution.py:41
  212.9 3.1 convolution_add_fusion.2
  216.0 1.9 copy.67
  226.2 2.7 fusion.72
  229.0 8.9 %bitcast_add_fusion.3 = f32[256,32,64]{0,2,1:T(8,128)} fusion(f32[256,32,64]{0,2,1:T(8,128)S(1)} %fusion.72, bf16[256,32,64]{0,2,1:T(8,128)(2,1)S(1)} %bitcast.116, f32[32,256]{1,0:T(8,128)S(1)} %copy.64, f32[256,256]{1,0:T(8,128)S(1)} %fusion.73, f32[32,256]{1,0:T(8,128)} %bitcast.126, pred[256,256]{1,0:T(8,128)(4,1)S(1)} %iota_compare_fusion.2, ...), kind=kOutput, calls=%fused_computation.14.clone.1 | convolution fusion | flops 1622147072 | bytes 5668864 | tf_op jit(solution)/shard_map/while/body/eval_jaxpr/hts,shp->thp/dot_general | solution.py:41
  237.8 3.1 convolution_add_fusion.2
  241.0 1.9 copy.67
  251.3 2.7 fusion.72
  254.0 8.9 %bitcast_add_fusion.3 = f32[256,32,64]{0,2,1:T(8,128)} fusion(f32[256,32,64]{0,2,1:T(8,128)S(1)} %fusion.72, bf16[256,32,64]{0,2,1:T(8,128)(2,1)S(1)} %bitcast.116, f32[32,256]{1,0:T(8,128)S(1)} %copy.64, f32[256,256]{1,0:T(8,128)S(1)} %fusion.73, f32[32,256]{1,0:T(8,128)} %bitcast.126, pred[256,256]{1,0:T(8,128)(4,1)S(1)} %iota_compare_fusion.2, ...), kind=kOutput, calls=%fused_computation.14.clone.1 | convolution fusion | flops 1622147072 | bytes 5668864 | tf_op jit(solution)/shard_map/while/body/eval_jaxpr/hts,shp->thp/dot_general | solution.py:41
  262.9 3.1 convolution_add_fusion.2
  269.6 75.5 %while.23 = (s32[]{:T(128)}, f32[32,64,128]{2,1,0:T(8,128)S(1)}, f32[32]{0:T(128)S(1)}, f32[32,64,128]{2,1,0:T(8,128)S(1)}, s32[]{:T(128)}) while((s32[]{:T(128)}, f32[32,64,128]{2,1,0:T(8,128)S(1)}, f32[32]{0:T(128)S(1)}, f32[32,64,128]{2,1,0:T(8,128)S(1)}, s32[]{:T(128)}) %tuple.54), condition=%wide.region_6.7_spmd, body=%wide.region_5.6_spmd.sunk | while | flops 524290 | bytes 7340261 | solution.py:98
  269.8 3.5 collective-permute-start
  273.2 21.8 %collective-permute-done = f32[32,64,128]{2,1,0:T(8,128)S(1)} collective-permute-done((f32[32,64,128]{2,1,0:T(8,128)S(1)}, f32[32,64,128]{2,1,0:T(8,128)S(1)}, u32[]{:S(2)}, u32[]{:S(2)}) %collective-permute-start) | collective-permute-done | bytes 1048608 | tf_op jit(solution)/shard_map/while/body/eval_jaxpr/ppermute | solution.py:16
  295.2 4.5 %collective-permute-start = (f32[32,64,128]{2,1,0:T(8,128)S(1)}, f32[32,64,128]{2,1,0:T(8,128)S(1)}, u32[]{:S(2)}, u32[]{:S(2)}) collective-permute-start(f32[32,64,128]{2,1,0:T(8,128)S(1)} %multiply_add_fusion.2), channel_id=1, source_target_pairs={{0,8},{8,16},{16,24},{1,9},{9,17},{17,25},{2,10},{10,18},{18,26},{... | collective-permute-start | bytes 3145736 | tf_op jit(solution)/shard_map/while/body/eval_jaxpr/ppermute | solution.py:16
  299.6 20.8 %collective-permute-done = f32[32,64,128]{2,1,0:T(8,128)S(1)} collective-permute-done((f32[32,64,128]{2,1,0:T(8,128)S(1)}, f32[32,64,128]{2,1,0:T(8,128)S(1)}, u32[]{:S(2)}, u32[]{:S(2)}) %collective-permute-start) | collective-permute-done | bytes 1048608 | tf_op jit(solution)/shard_map/while/body/eval_jaxpr/ppermute | solution.py:16
  320.7 4.5 %collective-permute-start = (f32[32,64,128]{2,1,0:T(8,128)S(1)}, f32[32,64,128]{2,1,0:T(8,128)S(1)}, u32[]{:S(2)}, u32[]{:S(2)}) collective-permute-start(f32[32,64,128]{2,1,0:T(8,128)S(1)} %multiply_add_fusion.2), channel_id=1, source_target_pairs={{0,8},{8,16},{16,24},{1,9},{9,17},{17,25},{2,10},{10,18},{18,26},{... | collective-permute-start | bytes 3145736 | tf_op jit(solution)/shard_map/while/body/eval_jaxpr/ppermute | solution.py:16
  325.1 19.9 %collective-permute-done = f32[32,64,128]{2,1,0:T(8,128)S(1)} collective-permute-done((f32[32,64,128]{2,1,0:T(8,128)S(1)}, f32[32,64,128]{2,1,0:T(8,128)S(1)}, u32[]{:S(2)}, u32[]{:S(2)}) %collective-permute-start) | collective-permute-done | bytes 1048608 | tf_op jit(solution)/shard_map/while/body/eval_jaxpr/ppermute | solution.py:16
  345.0 11.2 %broadcast_multiply_fusion = f32[2048,32,64]{0,2,1:T(8,128)} fusion(f32[2048,32]{0,1:T(8,128)S(1)} %bitcast.122, f32[32,64,128]{2,1,0:T(8,128)S(1)} %get-tuple-element.72, bf16[2048,256]{1,0:T(8,128)(2,1)} %copy-done), kind=kOutput, calls=%fused_computation.60 | convolution fusion | flops 6446645248 | bytes 18612224 | tf_op jit(solution)/shard_map/tn,hpn->thp/dot_general | solution.py:100
  356.3 17.6 %copy.35 = f32[2048,2048]{1,0:T(8,128)} copy(f32[2048,2048]{0,1:T(8,128)} %bitcast.117) | data formatting | bytes 33554432 | tf_op jit(solution)/shard_map/reshape | solution.py:102
  373.9 20.4 %multiply_reduce_fusion = (f32[2048]{0:T(1024)S(1)}, f32[2048,2048]{1,0:T(8,128)}) fusion(bf16[2048,2048]{1,0:T(8,128)(2,1)} %param.16, f32[2048,2048]{1,0:T(8,128)} %copy.35, f32[8,256,2048]{2,1,0:T(8,128)} %get-tuple-element.70), kind=kLoop, calls=%fused_computation.53 | loop fusion | flops 37746688 | bytes 58728448 | tf_op jit(solution)/shard_map/reduce_sum | solution.py:104
  394.3 13.8 %psum.7 = f32[2048]{0:T(1024)S(1)} all-reduce(f32[2048]{0:T(1024)S(1)} %get-tuple-element.142), channel_id=1, replica_groups=mesh['seq'=4,'mp'=8] {'mp'}, use_global_device_ids=true, to_apply=%region_10.11 | all-reduce | flops 2048 | bytes 16384 | tf_op jit(solution)/shard_map/psum | solution.py:104
  408.1 9.5 %multiply_convert_fusion = bf16[2048,2048]{1,0:T(8,128)(2,1)} fusion(f32[2048,2048]{1,0:T(8,128)} %get-tuple-element.143, f32[2048]{0:T(1024)S(1)} %add_rsqrt_fusion, f32[2048]{0:T(1024)S(1)} %copy-done.4), kind=kLoop, calls=%fused_computation.52 | loop fusion | flops 12582912 | bytes 25182208 | tf_op jit(solution)/shard_map/convert_element_type | solution.py:106
  (165 shorter events, 85.0 us)
Async XLA Ops:
  0.0 45.1 %copy-start.2 = (bf16[2048,256]{1,0:T(8,128)(2,1)S(1)}, bf16[2048,256]{1,0:T(8,128)(2,1)}, u32[]{:S(2)}) copy-start(bf16[2048,256]{1,0:T(8,128)(2,1)} %param.15) | copy-start | bytes 3145732
  0.0 49.8 %copy-start.3 = (f32[2048]{0:T(1024)S(1)}, f32[2048]{0:T(1024)}, u32[]{:S(2)}) copy-start(f32[2048]{0:T(1024)} %param.20) | copy-start | bytes 24580
  0.8 44.3 %collective-permute-start.2 = (bf16[3,256]{1,0:T(4,128)(2,1)S(1)}, bf16[3,256]{1,0:T(4,128)(2,1)S(1)}, u32[]{:S(2)}, u32[]{:S(2)}) collective-permute-start(bf16[3,256]{1,0:T(4,128)(2,1)S(1)} %slice.82), channel_id=1, source_target_pairs={{0,8},{8,16},{16,24},{1,9},{9,17},{17,25},{2,10},{10,18},{18,26},{... | collective-permute-start | bytes 4616 | tf_op jit(solution)/shard_map/ppermute | solution.py:16
  6.4 43.4 %collective-permute-start.1 = (bf16[3,2048]{1,0:T(4,128)(2,1)S(1)}, bf16[3,2048]{1,0:T(4,128)(2,1)S(1)}, u32[]{:S(2)}, u32[]{:S(2)}) collective-permute-start(bf16[3,2048]{1,0:T(4,128)(2,1)S(1)} %slice.74), channel_id=1, source_target_pairs={{0,8},{8,16},{16,24},{1,9},{9,17},{17,25},{2,10},{10,18},{18,26},{... | collective-permute-start | bytes 36872 | tf_op jit(solution)/shard_map/ppermute | solution.py:16
  47.3 1.0 copy-start
  269.5 75.6 %copy-start.1 = (f32[4,8,16,128]{3,1,2,0:T(8,128)S(1)}, f32[4,8,16,128]{3,1,2,0:T(8,128)}, u32[]{:S(2)}) copy-start(f32[4,8,16,128]{3,1,2,0:T(8,128)} %copy.53) | copy-start | bytes 786436
  269.8 25.2 %collective-permute-start = (f32[32,64,128]{2,1,0:T(8,128)S(1)}, f32[32,64,128]{2,1,0:T(8,128)S(1)}, u32[]{:S(2)}, u32[]{:S(2)}) collective-permute-start(f32[32,64,128]{2,1,0:T(8,128)S(1)} %multiply_add_fusion.2), channel_id=1, source_target_pairs={{0,8},{8,16},{16,24},{1,9},{9,17},{17,25},{2,10},{10,18},{18,26},{... | collective-permute-start | bytes 3145736 | tf_op jit(solution)/shard_map/while/body/eval_jaxpr/ppermute | solution.py:16
  295.2 25.3 %collective-permute-start = (f32[32,64,128]{2,1,0:T(8,128)S(1)}, f32[32,64,128]{2,1,0:T(8,128)S(1)}, u32[]{:S(2)}, u32[]{:S(2)}) collective-permute-start(f32[32,64,128]{2,1,0:T(8,128)S(1)} %multiply_add_fusion.2), channel_id=1, source_target_pairs={{0,8},{8,16},{16,24},{1,9},{9,17},{17,25},{2,10},{10,18},{18,26},{... | collective-permute-start | bytes 3145736 | tf_op jit(solution)/shard_map/while/body/eval_jaxpr/ppermute | solution.py:16
  320.7 24.4 %collective-permute-start = (f32[32,64,128]{2,1,0:T(8,128)S(1)}, f32[32,64,128]{2,1,0:T(8,128)S(1)}, u32[]{:S(2)}, u32[]{:S(2)}) collective-permute-start(f32[32,64,128]{2,1,0:T(8,128)S(1)} %multiply_add_fusion.2), channel_id=1, source_target_pairs={{0,8},{8,16},{16,24},{1,9},{9,17},{17,25},{2,10},{10,18},{18,26},{... | collective-permute-start | bytes 3145736 | tf_op jit(solution)/shard_map/while/body/eval_jaxpr/ppermute | solution.py:16
  373.9 34.3 %copy-start.4 = (f32[2048]{0:T(1024)S(1)}, f32[2048]{0:T(1024)}, u32[]{:S(2)}) copy-start(f32[2048]{0:T(1024)} %param.23) | copy-start | bytes 24580
where the time goes:
time: 422 us; the launch traced here: 418 us
  matrix products  140 us (33%)
  other arithmetic  91.2 us (22%)
  local copies, waits for them, and re-layouts  88.8 us (21%)
  waiting for transfers between devices  62.5 us (15%)
  starting transfers between devices  20.6 us (5%)
  blocking collectives  13.8 us (3%)
    dot_general x8, matrix products, block_pass(): jnp.einsum('hts,shp->thp', weights, per_head, precision=FULL_PRECISION)  70.8 us
    ppermute x5, waiting for transfers between devices, passed_along(): return lax.ppermute(block, axis, route)  62.5 us
    another operation x4, other arithmetic  27.3 us
    dynamic_update_slice x16, local copies, waits for them, and re-layouts, on_device(): local_end, local_out = lax.scan(block_pass, zero_state, inputs)  27.3 us
    dot_general x8, matrix products, block_pass(): jnp.einsum('shp,sn->hpn', weighted, input_map, precision=FULL_PRECISION)  25.1 us
    dynamic_slice x32, local copies, waits for them, and re-layouts, on_device(): local_end, local_out = lax.scan(block_pass, zero_state, inputs)  23.2 us
    dot_general x8, matrix products, block_pass(): jnp.einsum('tn,hpn->thp', output_map, state_now, precision=FULL_PRECISION)  21.9 us
    convert_element_type x2, other arithmetic, causal_mix(): return jax.nn.silu(running).astype(jnp.bfloat16)  21.6 us
  transfers between devices with their start and end apart: 5, of which 3 were waited for; matrix products, arithmetic and copies ran while one was open for 10% of the time, Pallas kernels for 0%

commit v1 on v0

v1 whole, which is shorter than its diff:
```python
import functools
import jax
import jax.numpy as jnp
from jax import lax
from jax.sharding import PartitionSpec as P
from jax.experimental import pallas as pl
from jax.experimental.pallas import tpu as pltpu

INNER = 16384
Q = 128
STATE = 128
HEAD = 64
LOG2E = 1.4426950408889634
F32 = jnp.float32
BF = jnp.bfloat16
HI = lax.Precision.HIGHEST
VMEM_LIMIT = 48 * 1024 * 1024


def iota(shape, dim):
    return lax.broadcasted_iota(jnp.int32, shape, dim)


def dot(a, b, **kw):
    return jnp.dot(a, b, preferred_element_type=F32, **kw)


def dot_rows(a, b, **kw):
    return lax.dot_general(a, b, (((1,), (1,)), ((), ())), preferred_element_type=F32, **kw)


def silu(v):
    return v * pl.reciprocal(1.0 + jnp.exp2(v * -LOG2E), approx=True)


def split3(v):
    hi = v.astype(BF).astype(F32)
    mid = (v - hi).astype(BF).astype(F32)
    return hi, mid, (v - hi) - mid


def expander(heads, width):
    row, col = iota((Q, width), 0), iota((Q, width), 1)
    hit = ((row & (heads - 1)) == (col >> 6)) & (row < 4 * heads)
    return jnp.where(hit, 1.0, 0.0).astype(BF)


def mix(tail, x, taps, bias):
    seen = jnp.concatenate([tail, x], axis=0)
    v = bias + taps[3:4] * x
    for back in (1, 2, 3):
        v = v + taps[3 - back : 4 - back] * pltpu.roll(seen, back, 0)[8:]
    return silu(v).astype(BF)


def states_kernel(
    feat, coup, raw, dlog, tapf, offf, tapc, offc, ftail, ctail,
    x_out, cb_out, m_out, lt_out, le_out, d_out, e_out,
    ex, ftl, ctl, acc, dec,
):
    c = pl.program_id(0)
    heads, width = raw.shape[0], feat.shape[1]

    @pl.when(c == 0)
    def _():
        ex[...] = expander(heads, width)
        ftl[...] = ftail[...]
        ctl[...] = ctail[...]
        acc[...] = jnp.zeros_like(acc)
        dec[...] = jnp.ones_like(dec)

    r = raw[...]
    step = jnp.maximum(r, 0.0) + jnp.log1p(jnp.exp(-jnp.abs(r)))
    ld = -jnp.exp(dlog[...]) * step * LOG2E
    upto = jnp.where(iota((Q, Q), 0) <= iota((Q, Q), 1), 1.0, 0.0)
    lc = dot(ld, upto, precision=HI)
    m = lc - jnp.log(step) * LOG2E
    m_out[...] = m
    to_end = jnp.exp2(lc[:, Q - 1 : Q] - m)
    parts = [to_end, *split3(jnp.exp2(lc))]
    if 4 * heads < Q:
        parts.append(jnp.zeros((Q - 4 * heads, Q), F32))
    t1 = jnp.transpose(jnp.concatenate(parts, axis=0))
    lane = iota((Q, Q), 1)
    lte = jnp.where(lane < heads, t1, 0.0).astype(BF)
    le = jnp.where(lane >= heads, t1, 0.0).astype(BF)
    le_out[...] = le
    lt_out[...] = jnp.transpose(jnp.concatenate([lc] * (Q // heads), axis=0))
    spread = jnp.concatenate([lte, le[Q - 16 :]], axis=0)

    halves = []
    for j in range(2):
        sl = slice(j * STATE, (j + 1) * STATE)
        x = coup[:, sl].astype(F32)
        f = mix(ctl[:, sl], x, tapc[:, sl], offc[:, sl])
        cb_out[:, sl] = f
        ctl[:, sl] = x[Q - 8 :]
        halves.append(f)
    bt = jnp.transpose(halves[0].astype(F32)).astype(BF)

    for j in range(width // 256):
        sl = slice(j * 256, (j + 1) * 256)
        x = feat[:, sl].astype(F32)
        f = mix(ftl[:, sl], x, tapf[:, sl], offf[:, sl])
        x_out[:, sl] = f
        ftl[:, sl] = x[Q - 8 :]
        e = dot(spread, ex[:, sl])
        xw = (f.astype(F32) * e[:Q]).astype(BF)
        d = dot(bt, xw)
        row = e[Q + 15 : Q + 16]
        d_out[:, sl] = d.astype(BF)
        acc[:, sl] = acc[:, sl] * row + d
        dec[:, sl] = dec[:, sl] * row

    @pl.when(c == pl.num_programs(0) - 1)
    def _():
        e_out[0:STATE] = acc[...].astype(BF)
        hi, mid, lo = split3(dec[...])
        which = iota(dec.shape, 0)
        rows = jnp.where(which == 0, hi, jnp.where(which == 1, mid, jnp.where(which == 2, lo, 0.0)))
        e_out[STATE : STATE + 16] = jnp.concatenate([rows, jnp.zeros_like(rows)], axis=0).astype(BF)


def inside_kernel(x_ref, cb, m, lt, y_out):
    scores = dot_rows(cb[:, STATE:], cb[:, :STATE])
    causal = iota((Q, Q), 0) >= iota((Q, Q), 1)
    first = jnp.where(iota((Q, Q), 1) < HEAD, 1.0, 0.0)
    mask_a, mask_b = first.astype(BF), (1.0 - first).astype(BF)
    for p in range(x_ref.shape[1] // 128):
        ws = []
        for h in (2 * p, 2 * p + 1):
            decay = jnp.exp2(lt[:, h : h + 1] - m[h : h + 1, :])
            ws.append((jnp.where(causal, decay, 0.0) * scores).astype(BF))
        xp = x_ref[:, p * 128 : (p + 1) * 128]
        both = jnp.concatenate([xp * mask_a, xp * mask_b], axis=0)
        y = dot(jnp.concatenate(ws, axis=1), both)
        y_out[:, p * 128 : (p + 1) * 128] = y.astype(BF)


def carried_kernel(heads, others, *refs):
    recv = refs[:others]
    d, le, cb, y_in, gate, g_out, ss_out, state, ex = refs[others:]
    width = gate.shape[1]

    @pl.when(pl.program_id(0) == 0)
    def _():
        ex[...] = expander(heads, width)
        if others == 0:
            state[...] = jnp.zeros_like(state)
        for j in range(width // 256 if others else 0):
            sl = slice(j * 256, (j + 1) * 256)
            total = jnp.zeros((STATE, 256), F32)
            through = jnp.ones((1, 256), F32)
            for r in recv:
                total = total + through * r[:STATE, sl].astype(F32)
                rows = r[STATE : STATE + 16, sl].astype(F32)
                through = through * (rows[0:1] + rows[1:2] + rows[2:3])
            state[:, sl] = total

    out_map = cb[:, STATE:]
    lev = le[...]
    acc = jnp.zeros((Q, 256), F32)
    for j in range(width // 256):
        sl = slice(j * 256, (j + 1) * 256)
        s = state[:, sl]
        e = dot(lev, ex[:, sl])
        y = y_in[:, sl].astype(F32) + dot(out_map, s.astype(BF)) * e
        g = y * silu(gate[:, sl].astype(F32))
        acc = acc + g * g
        g_out[:, sl] = g.astype(BF)
        state[:, sl] = s * e[Q - 1 : Q] + d[:, sl].astype(F32)
    acc = acc[:, :128] + acc[:, 128:]
    ss_out[0] = dot_rows(jnp.ones((8, Q), F32), acc, precision=HI)


def norm_kernel(ss, g, gain, out):
    c = pl.program_id(0)
    scale = lax.rsqrt(ss[pl.ds(c, 1), :] * (1.0 / INNER) + 1e-5)
    scale = jnp.transpose(jnp.broadcast_to(scale, (Q, Q)))
    for j in range(g.shape[1] // 128):
        sl = slice(j * 128, (j + 1) * 128)
        out[:, sl] = (g[:, sl].astype(F32) * gain[:, sl] * scale).astype(BF)


def passed_along(block, distance):
    devices = range(lax.axis_size("seq"))
    route = [(i - distance, i) for i in devices if i - distance in devices]
    return lax.ppermute(block, "seq", route)


def params():
    return pltpu.CompilerParams(vmem_limit_bytes=VMEM_LIMIT)


def on_device(
    features, coupling, gate_values, step_raw, decay_log,
    feature_taps, feature_offset, coupling_taps, coupling_offset, norm_gain,
):
    tokens, width = features.shape
    heads = decay_log.shape[0]
    blocks = tokens // Q
    seq = lax.axis_size("seq")
    tail = feature_taps.shape[0] - 1
    ends = jnp.concatenate([features[tokens - tail :], coupling[tokens - tail :]], axis=1)
    prior = passed_along(ends, 1)
    prior = jnp.pad(prior, ((8 - tail, 0), (0, 0))).astype(F32)

    def whole(*shape):
        return pl.BlockSpec(shape, lambda c: (0,) * len(shape))

    def rows(n):
        return pl.BlockSpec((Q, n), lambda c: (c, 0))

    cols = pl.BlockSpec((heads, Q), lambda c: (0, c))
    sds = jax.ShapeDtypeStruct
    work = 2 * tokens * width * STATE
    x, cb, m, lt, le, d, end = pl.pallas_call(
        states_kernel,
        grid=(blocks,),
        in_specs=[
            rows(width), rows(2 * STATE), cols, whole(heads, 1), whole(4, width), whole(1, width),
            whole(4, 2 * STATE), whole(1, 2 * STATE), whole(8, width), whole(8, 2 * STATE),
        ],
        out_specs=[
            rows(width), rows(2 * STATE), cols, rows(Q), rows(Q), rows(width),
            whole(STATE + 16, width),
        ],
        out_shape=[
            sds((tokens, width), BF), sds((tokens, 2 * STATE), BF), sds((heads, tokens), F32),
            sds((tokens, Q), F32), sds((tokens, Q), BF), sds((tokens, width), BF),
            sds((STATE + 16, width), BF),
        ],
        scratch_shapes=[
            pltpu.VMEM((Q, width), BF), pltpu.VMEM((8, width), F32),
            pltpu.VMEM((8, 2 * STATE), F32), pltpu.VMEM((STATE, width), F32),
            pltpu.VMEM((8, width), F32),
        ],
        compiler_params=params(),
        cost_estimate=pl.CostEstimate(flops=2 * work, bytes_accessed=6 * tokens * width, transcendentals=0),
        name="states",
    )(
        features, coupling, step_raw, decay_log[:, None], feature_taps, feature_offset[None],
        coupling_taps, coupling_offset[None], prior[:, :width], prior[:, width:],
    )
    recv = [passed_along(end, distance) for distance in range(1, seq)]
    y = pl.pallas_call(
        inside_kernel,
        grid=(blocks,),
        in_specs=[rows(width), rows(2 * STATE), cols, rows(Q)],
        out_specs=rows(width),
        out_shape=sds((tokens, width), BF),
        compiler_params=params(),
        cost_estimate=pl.CostEstimate(flops=8 * work, bytes_accessed=4 * tokens * width, transcendentals=0),
        name="inside",
    )(x, cb, m, lt)
    g, ss = pl.pallas_call(
        functools.partial(carried_kernel, heads, seq - 1),
        grid=(blocks,),
        in_specs=[whole(STATE + 16, width)] * (seq - 1)
        + [rows(width), rows(Q), rows(2 * STATE), rows(width), rows(width)],
        out_specs=[rows(width), pl.BlockSpec((1, 8, Q), lambda c: (c, 0, 0))],
        out_shape=[sds((tokens, width), BF), sds((blocks, 8, Q), F32)],
        scratch_shapes=[pltpu.VMEM((STATE, width), F32), pltpu.VMEM((Q, width), BF)],
        compiler_params=params(),
        cost_estimate=pl.CostEstimate(flops=2 * work, bytes_accessed=8 * tokens * width, transcendentals=0),
        name="carried",
    )(*recv, d, le, cb, y, gate_values)
    squares = lax.psum(ss[:, 0, :], "mp")
    return pl.pallas_call(
        norm_kernel,
        grid=(blocks,),
        in_specs=[whole(blocks, Q), rows(width), whole(1, width)],
        out_specs=rows(width),
        out_shape=sds((tokens, width), BF),
        compiler_params=params(),
        cost_estimate=pl.CostEstimate(flops=2 * tokens * width, bytes_accessed=4 * tokens * width, transcendentals=0),
        name="normalise",
    )(squares, g, norm_gain[None])


def solution(mesh):
    in_specs = (
        P("seq", "mp"), P("seq", None), P("seq", "mp"), P("mp", "seq"), P("mp"),
        P(None, "mp"), P("mp"), P(), P(), P("mp"),
    )
    return jax.shard_map(
        on_device, mesh=mesh, in_specs=in_specs, out_specs=P("seq", "mp"), check_vma=False
    )
```

time: 422 us -> 126 us (0.30)
  matrix products: 140 us -> 0 us
  other arithmetic: 91.2 us -> 0.03 us
  Pallas kernels: 0 us -> 83.1 us
  local copies, waits for them, and re-layouts: 88.8 us -> 7.22 us
  waiting for transfers between devices: 62.5 us -> 3.11 us
  starting transfers between devices: 20.6 us -> 13.8 us
    dot_general x33 -> x0, matrix products: 140 us -> none  [the longest x8 70.8 us: block_pass(): jnp.einsum('hts,shp->thp', weights, per_head, precision=FULL_PRECISION)]
    pallas_call x0 -> x4, Pallas kernels: none -> 83.1 us  [the longest x1 29.5 us: on_device(): pl.pallas_call(states_kernel, grid=(blocks,), in_specs=[rows(width), rows...]
    ppermute x5 -> x4, waiting for transfers between devices: 62.5 us -> 3.11 us  [passed_along(): return lax.ppermute(block, 'seq', route)]
    convert_element_type x3 -> x1, other arithmetic: 31.1 us -> 0.01 us  [on_device(): prior = jnp.pad(prior, ((8 - tail, 0), (0, 0))).astype(F32)]
    another operation x4 -> x0, other arithmetic: 27.3 us -> none
    dynamic_update_slice x16 -> x0, local copies, waits for them, and re-layouts: 27.3 us -> none  [on_device(): local_end, local_out = lax.scan(block_pass, zero_state, inputs)]
    dynamic_slice x32 -> x0, local copies, waits for them, and re-layouts: 23.2 us -> none  [on_device(): local_end, local_out = lax.scan(block_pass, zero_state, inputs)]
    reduce_sum x2 -> x0, other arithmetic: 21.6 us -> none  [the longest x1 20.4 us: on_device(): squares = lax.psum(jnp.sum(gated_values * gated_values, axis=1), 'mp')]
  transfers between devices with their start and end apart: 5 -> 4, of which waited for: 3 -> 2; matrix products, arithmetic and copies ran while one was open for 10% -> 1% of each run, Pallas kernels for 0% -> 15%
where the time goes in v1:
time: 126 us; the launch traced here: 124 us
  Pallas kernels  83.1 us (66%)
  blocking collectives  17.1 us (14%)
  starting transfers between devices  13.8 us (11%)
  local copies, waits for them, and re-layouts  7.22 us (6%)
  waiting for transfers between devices  3.11 us (2%)
    pallas_call x1, Pallas kernels, on_device(): pl.pallas_call(states_kernel, grid=(blocks,), in_specs=[rows(width), rows...  29.5 us
    pallas_call x1, Pallas kernels, on_device(): pl.pallas_call(functools.partial(carried_kernel, heads, seq - 1), grid=(b...  22.1 us
    pallas_call x1, Pallas kernels, on_device(): pl.pallas_call(inside_kernel, grid=(blocks,), in_specs=[rows(width), rows...  18.7 us
    psum x1, blocking collectives, on_device(): squares = lax.psum(ss[:, 0, :], 'mp')  17.1 us
    ppermute x4, starting transfers between devices, passed_along(): return lax.ppermute(block, 'seq', route)  13.8 us
    pallas_call x1, Pallas kernels, on_device(): pl.pallas_call(norm_kernel, grid=(blocks,), in_specs=[whole(blocks, Q), r...  12.8 us
    unnamed x14, local copies, waits for them, and re-layouts  4.99 us
    ppermute x4, waiting for transfers between devices, passed_along(): return lax.ppermute(block, 'seq', route)  3.11 us
  transfers between devices with their start and end apart: 4, of which 2 were waited for; matrix products, arithmetic and copies ran while one was open for 1% of the time, Pallas kernels for 15%

profile of v1, /device:TPU:0, one launch (start us, length us, event | category | flops | bytes accessed | tf_op | source)
XLA Modules:
  0.0 124.5 jit_solution(13027271780705277050)
XLA Ops:
  0.0 0.8 slice.15
  0.8 0.7 slice.16
  1.5 4.8 %collective-permute-start = (bf16[3,2304]{1,0:T(4,128)(2,1)S(1)}, bf16[3,2304]{1,0:T(4,128)(2,1)S(1)}, u32[]{:S(2)}, u32[]{:S(2)}) collective-permute-start(bf16[3,2304]{1,0:T(4,128)(2,1)S(1)} %pad_maximum_fusion), channel_id=1, source_target_pairs={{0,8},{8,16},{16,24},{1,9},{9,17},{17,25},{2,10},{10,18},{18,26},{... | collective-permute-start | bytes 41480 | tf_op jit(solution)/shard_map/ppermute | solution.py:188
  6.3 0.7 copy.11.dlog
  7.1 0.7 collective-permute-done
  7.8 0.0 copy-start
  7.8 1.2 copy-done
  9.1 0.0 copy-start.1
  9.1 0.9 copy-done.1
  10.0 0.0 copy-start.2
  10.0 0.8 copy-done.2
  10.8 0.0 copy-start.4
  10.8 0.7 copy-done.4
  11.5 0.0 copy-start.5
  11.5 0.7 copy-done.5
  12.1 0.0 copy-start.6
  12.1 0.7 copy-done.6
  12.8 29.5 %states.1 = (bf16[2048,2048]{1,0:T(8,128)(2,1)}, bf16[2048,256]{1,0:T(8,128)(2,1)S(1)}, f32[32,2048]{1,0:T(8,128)S(1)}, f32[2048,128]{1,0:T(8,128)S(1)}, bf16[20...) custom-call(bf16[2048,2048]{1,0:T(8,128)(2,1)} %feat.1, ...), custom_call_target="tpu_custom_call" | custom-call | flops 2147483648 | bytes 25165824 | tf_op jit(solution)/shard_map/states/pallas_call | solution.py:217
  42.4 4.2 %collective-permute-start.1 = (bf16[144,2048]{1,0:T(8,128)(2,1)S(1)}, bf16[144,2048]{1,0:T(8,128)(2,1)S(1)}, u32[]{:S(2)}, u32[]{:S(2)}) collective-permute-start(bf16[144,2048]{1,0:T(8,128)(2,1)S(1)} %get-tuple-element.14), channel_id=1, source_target_pairs={{0,8},{8,16},{16,24},{1,9},{9,17},{17,25},{2,10},{10,18},{18,26},{... | collective-permute-start | bytes 1769480 | tf_op jit(solution)/shard_map/ppermute | solution.py:188
  46.6 3.4 %collective-permute-start.2 = (bf16[144,2048]{1,0:T(8,128)(2,1)S(1)}, bf16[144,2048]{1,0:T(8,128)(2,1)S(1)}, u32[]{:S(2)}, u32[]{:S(2)}) collective-permute-start(bf16[144,2048]{1,0:T(8,128)(2,1)S(1)} %get-tuple-element.14), channel_id=1, source_target_pairs={{0,16},{8,24},{1,17},{9,25},{2,18},{10,26},{3,19},{11,27},{4,20},{... | collective-permute-start | bytes 1769480 | tf_op jit(solution)/shard_map/ppermute | solution.py:188
  50.0 1.3 %collective-permute-start.3 = (bf16[144,2048]{1,0:T(8,128)(2,1)S(1)}, bf16[144,2048]{1,0:T(8,128)(2,1)S(1)}, u32[]{:S(2)}, u32[]{:S(2)}) collective-permute-start(bf16[144,2048]{1,0:T(8,128)(2,1)S(1)} %get-tuple-element.14), channel_id=1, source_target_pairs={{0,24},{1,25},{2,26},{3,27},{4,28},{5,29},{6,30},{7,31}} | collective-permute-start | bytes 1769480 | tf_op jit(solution)/shard_map/ppermute | solution.py:188
  51.4 18.7 %inside.1.refs_6_ = bf16[2048,2048]{1,0:T(8,128)(2,1)} custom-call(bf16[2048,2048]{1,0:T(8,128)(2,1)} %get-tuple-element.18.x_ref, bf16[2048,256]{1,0:T(8,128)(2,1)S(1)} %get-tuple-element.17.cb.refs_5_, f32[32,2048]{1,0:T(8,128)S(1)} %get-tuple-element.19.m, f32[2048,128]{1,0:T(8,128)S(1)} %get-tuple-element.20.lt), custom_call_target="tpu_custom_call" | custom-call | flops 8589934592 | bytes 16777216 | tf_op jit(solution)/shard_map/inside/pallas_call | solution.py:246
  70.0 0.0 collective-permute-done.1.refs_0_
  70.0 2.4 %collective-permute-done.2.refs_1_ = bf16[144,2048]{1,0:T(8,128)(2,1)S(1)} collective-permute-done((bf16[144,2048]{1,0:T(8,128)(2,1)S(1)}, bf16[144,2048]{1,0:T(8,128)(2,1)S(1)}, u32[]{:S(2)}, u32[]{:S(2)}) %collective-permute-start.2) | collective-permute-done | bytes 589856 | tf_op jit(solution)/shard_map/ppermute | solution.py:188
  72.4 0.0 collective-permute-done.3.refs_2_
  72.4 0.0 copy-start.3
  72.4 22.1 %carried.1 = (bf16[2048,2048]{1,0:T(8,128)(2,1)}, f32[16,8,128]{2,1,0:T(8,128)S(1)}) custom-call(bf16[144,2048]{1,0:T(8,128)(2,1)S(1)} %collective-permute-done.1.refs_0_, bf16[144,2048]{1,0:T(8,128)(2,1)S(1)} %collective-permute-done.2.refs_1_, bf16[144,2048]{1,0:T(8,128)(2,1)S(1)} %collective-permute-done.3.refs_2_, ...), custom_call_target="tpu_custom_call" | custom-call | flops 2147483648 | bytes 33554432 | tf_op jit(solution)/shard_map/carried/pallas_call | solution.py:256
  94.6 17.1 %psum.7.ss = f32[16,128]{1,0:T(8,128)S(1)} all-reduce(f32[16,128]{1,0:T(8,128)S(1)} %slice_bitcast_fusion), channel_id=1, replica_groups=mesh['seq'=4,'mp'=8] {'mp'}, use_global_device_ids=true, to_apply=%region_0.1 | all-reduce | flops 2048 | bytes 16384 | tf_op jit(solution)/shard_map/psum | solution.py:268
  111.6 0.0 copy-done.3
  111.6 12.8 %normalise.1 = bf16[2048,2048]{1,0:T(8,128)(2,1)} custom-call(f32[16,128]{1,0:T(8,128)S(1)} %psum.7.ss, bf16[2048,2048]{1,0:T(8,128)(2,1)} %get-tuple-element.22.g, f32[1,2048]{1,0:T(1,128)S(1)} %bitcast.6), custom_call_target="tpu_custom_call" | custom-call | flops 8388608 | bytes 16777216 | tf_op jit(solution)/shard_map/normalise/pallas_call | solution.py:269
  (6 shorter events, 0.1 us)
Async XLA Ops:
  1.5 6.3 %collective-permute-start = (bf16[3,2304]{1,0:T(4,128)(2,1)S(1)}, bf16[3,2304]{1,0:T(4,128)(2,1)S(1)}, u32[]{:S(2)}, u32[]{:S(2)}) collective-permute-start(bf16[3,2304]{1,0:T(4,128)(2,1)S(1)} %pad_maximum_fusion), channel_id=1, source_target_pairs={{0,8},{8,16},{16,24},{1,9},{9,17},{17,25},{2,10},{10,18},{18,26},{... | collective-permute-start | bytes 41480 | tf_op jit(solution)/shard_map/ppermute | solution.py:188
  7.8 1.2 copy-start
  9.1 0.9 copy-start.1
  10.0 0.8 copy-start.2
  10.8 0.7 copy-start.4
  11.5 0.7 copy-start.5
  12.1 0.7 copy-start.6
  42.4 27.7 %collective-permute-start.1 = (bf16[144,2048]{1,0:T(8,128)(2,1)S(1)}, bf16[144,2048]{1,0:T(8,128)(2,1)S(1)}, u32[]{:S(2)}, u32[]{:S(2)}) collective-permute-start(bf16[144,2048]{1,0:T(8,128)(2,1)S(1)} %get-tuple-element.14), channel_id=1, source_target_pairs={{0,8},{8,16},{16,24},{1,9},{9,17},{17,25},{2,10},{10,18},{18,26},{... | collective-permute-start | bytes 1769480 | tf_op jit(solution)/shard_map/ppermute | solution.py:188
  46.6 25.8 %collective-permute-start.2 = (bf16[144,2048]{1,0:T(8,128)(2,1)S(1)}, bf16[144,2048]{1,0:T(8,128)(2,1)S(1)}, u32[]{:S(2)}, u32[]{:S(2)}) collective-permute-start(bf16[144,2048]{1,0:T(8,128)(2,1)S(1)} %get-tuple-element.14), channel_id=1, source_target_pairs={{0,16},{8,24},{1,17},{9,25},{2,18},{10,26},{3,19},{11,27},{4,20},{... | collective-permute-start | bytes 1769480 | tf_op jit(solution)/shard_map/ppermute | solution.py:188
  50.0 22.4 %collective-permute-start.3 = (bf16[144,2048]{1,0:T(8,128)(2,1)S(1)}, bf16[144,2048]{1,0:T(8,128)(2,1)S(1)}, u32[]{:S(2)}, u32[]{:S(2)}) collective-permute-start(bf16[144,2048]{1,0:T(8,128)(2,1)S(1)} %get-tuple-element.14), channel_id=1, source_target_pairs={{0,24},{1,25},{2,26},{3,27},{4,28},{5,29},{6,30},{7,31}} | collective-permute-start | bytes 1769480 | tf_op jit(solution)/shard_map/ppermute | solution.py:188
  72.4 39.2 %copy-start.3 = (f32[2048]{0:T(1024)S(1)}, f32[2048]{0:T(1024)}, u32[]{:S(2)}) copy-start(f32[2048]{0:T(1024)} %param.19) | copy-start | bytes 24580

commit v2 on v1

v2 whole, which is shorter than its diff:
```python
import functools
import jax
import jax.numpy as jnp
from jax import lax
from jax.sharding import PartitionSpec as P
from jax.experimental import pallas as pl
from jax.experimental.pallas import tpu as pltpu

INNER = 16384
Q = 128
ROWS = 512
STATE = 128
HEAD = 64
LOG2E = 1.4426950408889634
F32 = jnp.float32
BF = jnp.bfloat16
HI = lax.Precision.HIGHEST
VMEM_LIMIT = 60 * 1024 * 1024


def iota(shape, dim):
    return lax.broadcasted_iota(jnp.int32, shape, dim)


def dot(a, b, **kw):
    return jnp.dot(a, b, preferred_element_type=F32, **kw)


def dot_rows(a, b, **kw):
    return lax.dot_general(a, b, (((1,), (1,)), ((), ())), preferred_element_type=F32, **kw)


def silu(v):
    return v * pl.reciprocal(1.0 + jnp.exp2(v * -LOG2E), approx=True)


def split3(v):
    hi = v.astype(BF).astype(F32)
    mid = (v - hi).astype(BF).astype(F32)
    return hi, mid, (v - hi) - mid


def expander(heads, width, first_head):
    row, col = iota((Q, width), 0), iota((Q, width), 1)
    hit = ((row & (heads - 1)) == (col >> 6) + first_head) & (row < 4 * heads)
    return jnp.where(hit, 1.0, 0.0).astype(BF)


def mix(tail, x, taps, bias):
    seen = jnp.concatenate([tail, x], axis=0)
    v = bias + taps[3:4] * x
    for back in (1, 2, 3):
        v = v + taps[3 - back : 4 - back] * pltpu.roll(seen, back, 0)[8:]
    return silu(v).astype(BF)


def prepare_kernel(raw, dlog, m_out, lt_out, le_out, lte_out):
    heads, tokens = raw.shape
    blocks = tokens // Q
    r = jnp.concatenate([raw[:, c * Q : (c + 1) * Q] for c in range(blocks)], axis=0)
    step = jnp.maximum(r, 0.0) + jnp.log1p(jnp.exp(-jnp.abs(r)))
    rate = jnp.broadcast_to(jnp.exp(dlog[...]) * -LOG2E, (heads, Q))
    ld = jnp.concatenate([rate] * blocks, axis=0) * step
    upto = jnp.where(iota((Q, Q), 0) <= iota((Q, Q), 1), 1.0, 0.0)
    lc = dot(ld, upto, precision=HI)
    m = lc - jnp.log(step) * LOG2E
    to_end = jnp.exp2(lc[:, Q - 1 : Q] - m)
    pieces = split3(jnp.exp2(lc))
    lane = iota((Q, Q), 1)
    for c in range(blocks):
        sl, rs = slice(c * Q, (c + 1) * Q), slice(c * heads, (c + 1) * heads)
        m_out[:, sl] = m[rs]
        parts = [to_end[rs], *(piece[rs] for piece in pieces)]
        if 4 * heads < Q:
            parts.append(jnp.zeros((Q - 4 * heads, Q), F32))
        t1 = jnp.transpose(jnp.concatenate(parts, axis=0))
        lte_out[sl] = jnp.where(lane < heads, t1, 0.0).astype(BF)
        le_out[sl] = jnp.where(lane >= heads, t1, 0.0).astype(BF)
        lt_out[sl] = jnp.transpose(jnp.concatenate([lc[rs]] * (Q // heads), axis=0))


def exchange(n, src, dst, send_sem, recv_sem):
    me = lax.axis_index("seq")

    def copy(d):
        return pltpu.make_async_remote_copy(
            src_ref=src, dst_ref=dst.at[d - 1], send_sem=send_sem.at[d - 1], recv_sem=recv_sem.at[d - 1],
            device_id={"seq": lax.rem(me + d, n)}, device_id_type=pl.DeviceIdType.MESH,
        )

    @pl.when(pl.program_id(0) == 0)
    def _():
        barrier = pltpu.get_barrier_semaphore()
        for d in range(1, n):
            pl.semaphore_signal(
                barrier, inc=1, device_id={"seq": lax.rem(me + d, n)}, device_id_type=pl.DeviceIdType.MESH
            )
        pl.semaphore_wait(barrier, n - 1)
        for d in range(1, n):
            pl.when(me + d < n)(lambda d=d: copy(d).start())

    def finish():
        @pl.when(pl.program_id(0) == pl.num_programs(0) - 1)
        def _():
            for d in range(1, n):
                pl.when(me + d < n)(lambda d=d: copy(d).wait_send())
                pl.when(me >= d)(lambda d=d: copy(d).wait_recv())

    return finish


def chunks(ref):
    return ref.shape[0] // Q


def rows_of(i):
    return pl.ds(pl.multiple_of(i * Q, Q), Q)


def states_body(first_head, heads, feat, lte, le, taps, off, ftail, input_map, x_out, d_out, e_out, ex, ftl, acc, dec):
    c = pl.program_id(0)
    width = feat.shape[1]

    @pl.when(c == 0)
    def _():
        ex[...] = expander(heads, width, first_head)
        ftl[...] = ftail[...]
        acc[...] = jnp.zeros_like(acc)
        dec[...] = jnp.ones_like(dec)

    def one(i, carry):
        rs = rows_of(i)
        bt = jnp.transpose(input_map(rs).astype(F32)).astype(BF)
        ends = le[pl.ds(pl.multiple_of(i * Q + Q - 16, 16), 16), :]
        spread = jnp.concatenate([lte[rs, :], ends], axis=0)
        for j in range(width // 256):
            sl = slice(j * 256, (j + 1) * 256)
            e = dot(spread, ex[:, sl])
            xw = []
            for k in range(2):
                at = slice(j * 256 + k * 128, j * 256 + (k + 1) * 128)
                x = feat[rs, at].astype(F32)
                f = mix(ftl[:, at], x, taps[:, at], off[:, at])
                x_out[rs, at] = f
                ftl[:, at] = x[Q - 8 :]
                xw.append((f.astype(F32) * e[:Q, k * 128 : (k + 1) * 128]).astype(BF))
            d = dot(bt, jnp.concatenate(xw, axis=1))
            row = e[Q + 15 : Q + 16]
            d_out[rs, sl] = d.astype(BF)
            acc[:, sl] = acc[:, sl] * row + d
            dec[:, sl] = dec[:, sl] * row
        return carry

    lax.fori_loop(0, chunks(feat), one, 0)

    @pl.when(c == pl.num_programs(0) - 1)
    def _():
        e_out[0:STATE] = acc[...].astype(BF)
        hi, mid, lo = split3(dec[...])
        which = iota(dec.shape, 0)
        rows = jnp.where(which == 0, hi, jnp.where(which == 1, mid, jnp.where(which == 2, lo, 0.0)))
        e_out[STATE : STATE + 16] = jnp.concatenate([rows, jnp.zeros_like(rows)], axis=0).astype(BF)


def states_a_kernel(
    heads, feat, lte, le, taps, off, ftail, coup, tapc, offc, ctail, x_out, d_out, e_out, cb_out, ex, ftl, acc, dec, ctl
):
    @pl.when(pl.program_id(0) == 0)
    def _():
        ctl[...] = ctail[...]

    def input_map(rs):
        for j in (1, 0):
            sl = slice(j * STATE, (j + 1) * STATE)
            x = coup[rs, sl].astype(F32)
            f = mix(ctl[:, sl], x, tapc[:, sl], offc[:, sl])
            cb_out[rs, sl] = f
            ctl[:, sl] = x[Q - 8 :]
        return f

    states_body(0, heads, feat, lte, le, taps, off, ftail, input_map, x_out, d_out, e_out, ex, ftl, acc, dec)


def states_b_kernel(
    heads, n, feat, lte, le, taps, off, ftail, cb, e_a, x_out, d_out, e_out, recv, ex, ftl, acc, dec, send_sem, recv_sem
):
    finish = exchange(n, e_a, recv, send_sem, recv_sem)
    states_body(
        heads // 2, heads, feat, lte, le, taps, off, ftail, lambda rs: cb[rs, :STATE],
        x_out, d_out, e_out, ex, ftl, acc, dec,
    )
    finish()


def inside_kernel(n, x_a, x_b, cb, m, lt, e_b, y_out, recv, send_sem, recv_sem):
    finish = exchange(n, e_b, recv, send_sem, recv_sem)
    causal = iota((Q, Q), 0) >= iota((Q, Q), 1)
    first = jnp.where(iota((Q, Q), 1) < HEAD, 1.0, 0.0)
    mask_a, mask_b = first.astype(BF), (1.0 - first).astype(BF)
    half = x_a.shape[1] // 128

    def one(i, carry):
        rs = rows_of(i)
        scores = dot_rows(cb[rs, STATE:], cb[rs, :STATE])
        for p in range(2 * half):
            ws = []
            for h in (2 * p, 2 * p + 1):
                decay = jnp.exp2(lt[rs, h : h + 1] - m[h : h + 1, rs])
                ws.append((jnp.where(causal, decay, 0.0) * scores).astype(BF))
            x = x_a if p < half else x_b
            xp = x[rs, (p % half) * 128 : (p % half + 1) * 128]
            both = jnp.concatenate([xp * mask_a, xp * mask_b], axis=0)
            y = dot(jnp.concatenate(ws, axis=1), both)
            y_out[rs, p * 128 : (p + 1) * 128] = y.astype(BF)
        return carry

    lax.fori_loop(0, chunks(x_a), one, 0)
    finish()


def carried_kernel(heads, others, place, recv_a, recv_b, d_a, d_b, le, cb, y_in, gate, g_out, ss_out, state, ex):
    width = gate.shape[1]
    half = width // 2
    c = pl.program_id(0)

    @pl.when(c == 0)
    def _():
        ex[...] = expander(heads, width, 0)
        for j in range(width // 256):
            recv, at = (recv_a, j * 256) if j * 256 < half else (recv_b, j * 256 - half)
            total = jnp.zeros((STATE, 256), F32)
            through = jnp.ones((1, 256), F32)
            for d in range(others):
                came = place[0] > d
                end = recv[d, :STATE, at : at + 256].astype(F32)
                rows = recv[d, STATE : STATE + 16, at : at + 256].astype(F32)
                total = total + jnp.where(came, through * end, 0.0)
                through = jnp.where(came, through * (rows[0:1] + rows[1:2] + rows[2:3]), 0.0)
            state[:, j * 256 : (j + 1) * 256] = total

    def one(i, carry):
        rs = rows_of(i)
        out_map = cb[rs, STATE:]
        lev = le[rs, :]
        acc = jnp.zeros((Q, 128), F32)
        for j in range(width // 256):
            sl = slice(j * 256, (j + 1) * 256)
            d, at = (d_a, j * 256) if j * 256 < half else (d_b, j * 256 - half)
            s = state[:, sl]
            e = dot(lev, ex[:, sl])
            new = dot(out_map, s.astype(BF)) * e
            state[:, sl] = s * e[Q - 1 : Q] + d[rs, at : at + 256].astype(F32)
            for k in range(2):
                part = slice(j * 256 + k * 128, j * 256 + (k + 1) * 128)
                y = y_in[rs, part].astype(F32) + new[:, k * 128 : (k + 1) * 128]
                g = y * silu(gate[rs, part].astype(F32))
                acc = acc + g * g
                g_out[rs, part] = g.astype(BF)
        ss = dot_rows(jnp.ones((8, Q), F32), acc, precision=HI)
        ss_out[pl.ds(c * chunks(gate) + i, 1), :] = ss[0:1]
        return carry

    lax.fori_loop(0, chunks(gate), one, 0)


def sums_kernel(n, ss, out, slots, send_sem, recv_sem):
    me = lax.axis_index("mp")

    def copy(d):
        return pltpu.make_async_remote_copy(
            src_ref=ss, dst_ref=slots.at[d - 1], send_sem=send_sem.at[d - 1], recv_sem=recv_sem.at[d - 1],
            device_id={"mp": lax.rem(me + d, n)}, device_id_type=pl.DeviceIdType.MESH,
        )

    barrier = pltpu.get_barrier_semaphore()
    for d in range(1, n):
        pl.semaphore_signal(
            barrier, inc=1, device_id={"mp": lax.rem(me + d, n)}, device_id_type=pl.DeviceIdType.MESH
        )
    pl.semaphore_wait(barrier, n - 1)
    for d in range(1, n):
        copy(d).start()
    total = ss[...]
    for d in range(1, n):
        copy(d).wait()
        total = total + slots[d - 1]
    out[...] = total


def norm_kernel(ss, g, gain, out):
    c = pl.program_id(0)

    def one(i, carry):
        rs = rows_of(i)
        scale = lax.rsqrt(ss[pl.ds(c * chunks(g) + i, 1), :] * (1.0 / INNER) + 1e-5)
        scale = jnp.transpose(jnp.broadcast_to(scale, (Q, Q)))
        for j in range(g.shape[1] // 128):
            sl = slice(j * 128, (j + 1) * 128)
            out[rs, sl] = (g[rs, sl].astype(F32) * gain[:, sl] * scale).astype(BF)
        return carry

    lax.fori_loop(0, chunks(g), one, 0)


def passed_along(block, distance):
    devices = range(lax.axis_size("seq"))
    route = [(i - distance, i) for i in devices if i - distance in devices]
    return lax.ppermute(block, "seq", route)


def params(**kw):
    return pltpu.CompilerParams(vmem_limit_bytes=VMEM_LIMIT, **kw)


def on_device(
    features, coupling, gate_values, step_raw, decay_log,
    feature_taps, feature_offset, coupling_taps, coupling_offset, norm_gain,
):
    tokens, width = features.shape
    heads = decay_log.shape[0]
    blocks = tokens // Q
    grid = (tokens // ROWS,)
    half = width // 2
    seq, mp = lax.axis_size("seq"), lax.axis_size("mp")
    tail = feature_taps.shape[0] - 1
    ends = jnp.concatenate([features[tokens - tail :], coupling[tokens - tail :]], axis=1)
    prior = passed_along(ends, 1)
    prior = jnp.pad(prior, ((8 - tail, 0), (0, 0))).astype(F32)

    def whole(*shape):
        return pl.BlockSpec(shape, lambda c: (0,) * len(shape))

    def rows(n, at=0):
        return pl.BlockSpec((ROWS, n), lambda c: (c, at))

    def side(n, at):
        return pl.BlockSpec((n, half), lambda c: (0, at))

    hbm = pl.BlockSpec(memory_space=pl.ANY)
    vmem = pl.BlockSpec(memory_space=pltpu.VMEM)
    sds = jax.ShapeDtypeStruct
    work = 2 * tokens * width * STATE

    def cost(flops, moved):
        return pl.CostEstimate(flops=flops, bytes_accessed=moved * tokens * width, transcendentals=0)

    m, lt, le, lte = pl.pallas_call(
        prepare_kernel,
        in_specs=[vmem, vmem],
        out_specs=[vmem] * 4,
        out_shape=[
            sds((heads, tokens), F32), sds((tokens, Q), F32), sds((tokens, Q), BF), sds((tokens, Q), BF),
        ],
        compiler_params=params(),
        cost_estimate=pl.CostEstimate(flops=work // 64, bytes_accessed=tokens * 1024, transcendentals=0),
        name="prepare",
    )(step_raw, decay_log[:, None])

    part = sds((tokens, half), BF)
    end_shape = sds((STATE + 16, half), BF)
    recv_shape = sds((seq - 1, STATE + 16, half), BF)
    keep = [
        pltpu.VMEM((Q, half), BF), pltpu.VMEM((8, half), F32),
        pltpu.VMEM((STATE, half), F32), pltpu.VMEM((8, half), F32),
    ]
    sems = [pltpu.SemaphoreType.DMA((seq - 1,)), pltpu.SemaphoreType.DMA((seq - 1,))]

    def state_specs(at):
        return [rows(half, at), rows(Q), rows(Q), side(4, at), side(1, at), side(8, at)]

    state_args = (features, lte, le, feature_taps, feature_offset[None], prior)
    x_a, d_a, e_a, cb = pl.pallas_call(
        functools.partial(states_a_kernel, heads),
        grid=grid,
        in_specs=state_specs(0)
        + [rows(2 * STATE), whole(4, 2 * STATE), whole(1, 2 * STATE), pl.BlockSpec((8, 2 * STATE), lambda c: (0, width // (2 * STATE)))],
        out_specs=[rows(half), rows(half), whole(STATE + 16, half), rows(2 * STATE)],
        out_shape=[part, part, end_shape, sds((tokens, 2 * STATE), BF)],
        scratch_shapes=keep + [pltpu.VMEM((8, 2 * STATE), F32)],
        compiler_params=params(),
        cost_estimate=cost(work, 3),
        name="states_a",
    )(*state_args, coupling, coupling_taps, coupling_offset[None], prior)
    x_b, d_b, e_b, recv_a = pl.pallas_call(
        functools.partial(states_b_kernel, heads, seq),
        grid=grid,
        in_specs=state_specs(1) + [rows(2 * STATE), hbm],
        out_specs=[rows(half), rows(half), whole(STATE + 16, half), hbm],
        out_shape=[part, part, end_shape, recv_shape],
        scratch_shapes=keep + sems,
        compiler_params=params(collective_id=0, has_side_effects=True),
        cost_estimate=cost(work, 3),
        name="states_b",
    )(*state_args, cb, e_a)
    y, recv_b = pl.pallas_call(
        functools.partial(inside_kernel, seq),
        grid=grid,
        in_specs=[rows(half), rows(half), rows(2 * STATE), pl.BlockSpec((heads, ROWS), lambda c: (0, c)), rows(Q), hbm],
        out_specs=[rows(width), hbm],
        out_shape=[sds((tokens, width), BF), recv_shape],
        scratch_shapes=sems,
        compiler_params=params(collective_id=1, has_side_effects=True),
        cost_estimate=cost(4 * work, 4),
        name="inside",
    )(x_a, x_b, cb, m, lt, e_b)
    g, ss = pl.pallas_call(
        functools.partial(carried_kernel, heads, seq - 1),
        grid=grid,
        in_specs=[
            pl.BlockSpec(memory_space=pltpu.SMEM),
            whole(seq - 1, STATE + 16, half), whole(seq - 1, STATE + 16, half),
            rows(half), rows(half), rows(Q), rows(2 * STATE), rows(width), rows(width),
        ],
        out_specs=[rows(width), whole(blocks, Q)],
        out_shape=[sds((tokens, width), BF), sds((blocks, Q), F32)],
        scratch_shapes=[pltpu.VMEM((STATE, width), F32), pltpu.VMEM((Q, width), BF)],
        compiler_params=params(),
        cost_estimate=cost(2 * work, 8),
        name="carried",
    )(lax.axis_index("seq").reshape(1), recv_a, recv_b, d_a, d_b, le, cb, y, gate_values)
    squares = pl.pallas_call(
        functools.partial(sums_kernel, mp),
        in_specs=[vmem],
        out_specs=vmem,
        out_shape=sds((blocks, Q), F32),
        scratch_shapes=[
            pltpu.VMEM((mp - 1, blocks, Q), F32),
            pltpu.SemaphoreType.DMA((mp - 1,)), pltpu.SemaphoreType.DMA((mp - 1,)),
        ],
        compiler_params=params(collective_id=2, has_side_effects=True),
        name="sums",
    )(ss)
    return pl.pallas_call(
        norm_kernel,
        grid=grid,
        in_specs=[whole(blocks, Q), rows(width), whole(1, width)],
        out_specs=rows(width),
        out_shape=sds((tokens, width), BF),
        compiler_params=params(),
        cost_estimate=cost(2 * tokens * width, 4),
        name="normalise",
    )(squares, g, norm_gain[None])


def solution(mesh):
    in_specs = (
        P("seq", "mp"), P("seq", None), P("seq", "mp"), P("mp", "seq"), P("mp"),
        P(None, "mp"), P("mp"), P(), P(), P("mp"),
    )
    return jax.shard_map(
        on_device, mesh=mesh, in_specs=in_specs, out_specs=P("seq", "mp"), check_vma=False
    )
```

time: 126 us -> 108 us (0.86)
  blocking collectives: 17.1 us -> 0 us
  Pallas kernels: 83.1 us -> 98.8 us
  starting transfers between devices: 13.8 us -> 4.84 us
  local copies, waits for them, and re-layouts: 7.22 us -> 2.81 us
  waiting for transfers between devices: 3.11 us -> 0.01 us
    psum x1 -> x0, blocking collectives: 17.1 us -> none  [on_device(): squares = lax.psum(ss[:, 0, :], 'mp')]
    pallas_call x4 -> x7, Pallas kernels: 83.1 us -> 98.8 us  [the longest x1 23.8 us: on_device(): pl.pallas_call(functools.partial(carried_kernel, heads, seq - 1), grid=gr...]
    ppermute x4 -> x1, starting transfers between devices: 13.8 us -> 4.84 us  [passed_along(): return lax.ppermute(block, 'seq', route)]
    unnamed x14 -> x0, local copies, waits for them, and re-layouts: 4.99 us -> none
    ppermute x4 -> x1, waiting for transfers between devices: 3.11 us -> 0.01 us  [passed_along(): return lax.ppermute(block, 'seq', route)]
  transfers between devices with their start and end apart: 4 -> 1, of which waited for: 2 -> 0; matrix products, arithmetic and copies ran while one was open for 1% -> 1% of each run, Pallas kernels for 15% -> 3%
where the time goes in v2:
time: 108 us; the launch traced here: 107 us
  Pallas kernels  98.8 us (91%)
  starting transfers between devices  4.84 us (4%)
  local copies, waits for them, and re-layouts  2.81 us (3%)
    pallas_call x1, Pallas kernels, on_device(): pl.pallas_call(functools.partial(carried_kernel, heads, seq - 1), grid=gr...  23.8 us
    pallas_call x1, Pallas kernels, on_device(): pl.pallas_call(functools.partial(inside_kernel, seq), grid=grid, in_specs...  19 us
    pallas_call x1, Pallas kernels, on_device(): pl.pallas_call(functools.partial(states_b_kernel, heads, seq), grid=grid,...  18.8 us
    pallas_call x1, Pallas kernels, on_device(): pl.pallas_call(functools.partial(states_a_kernel, heads), grid=grid, in_s...  18.2 us
    pallas_call x1, Pallas kernels, on_device(): pl.pallas_call(norm_kernel, grid=grid, in_specs=[whole(blocks, Q), rows(w...  8.05 us
    pallas_call x1, Pallas kernels, on_device(): pl.pallas_call(functools.partial(sums_kernel, mp), in_specs=[vmem], out_s...  7.55 us
    ppermute x1, starting transfers between devices, passed_along(): return lax.ppermute(block, 'seq', route)  4.84 us
    pallas_call x1, Pallas kernels, on_device(): pl.pallas_call(prepare_kernel, in_specs=[vmem, vmem], out_specs=[vmem] *...  3.4 us
  transfers between devices with their start and end apart: 1, of which 0 were waited for; matrix products, arithmetic and copies ran while one was open for 1% of the time, Pallas kernels for 3%

profile of v2, /device:TPU:0, one launch (start us, length us, event | category | flops | bytes accessed | tf_op | source)
XLA Modules:
  0.0 107.2 jit_solution(6656693821757279458)
XLA Ops:
  0.0 0.8 slice.6
  0.8 0.7 slice.7
  1.5 4.8 %collective-permute-start = (bf16[3,2304]{1,0:T(4,128)(2,1)S(1)}, bf16[3,2304]{1,0:T(4,128)(2,1)S(1)}, u32[]{:S(2)}, u32[]{:S(2)}) collective-permute-start(bf16[3,2304]{1,0:T(4,128)(2,1)S(1)} %pad_maximum_fusion), channel_id=1, source_target_pairs={{0,8},{8,16},{16,24},{1,9},{9,17},{17,25},{2,10},{10,18},{18,26},{... | collective-permute-start | bytes 41480 | tf_op jit(solution)/shard_map/ppermute | solution.py:308
  6.3 1.3 %copy.11.dlog = f32[32,1]{1,0:T(8,128)} copy(f32[32,1]{0,1:T(1,128)} %bitcast.9) | data formatting | bytes 256 | tf_op jit(solution)/shard_map/broadcast_in_dim | solution.py:357
  7.7 3.4 %prepare.1 = (f32[32,2048]{1,0:T(8,128)}, f32[2048,128]{1,0:T(8,128)}, bf16[2048,128]{1,0:T(8,128)(2,1)}, bf16[2048,128]{1,0:T(8,128)(2,1)}) custom-call(f32[32,2048]{1,0:T(8,128)} %raw.1, f32[32,1]{1,0:T(8,128)} %copy.11.dlog), custom_call_target="tpu_custom_call" | custom-call | flops 16777216 | bytes 2097152 | tf_op jit(solution)/shard_map/prepare/pallas_call | solution.py:347
  11.1 0.0 collective-permute-done
  11.1 0.6 pad_convert_fusion.ftail.ctail
  11.7 18.2 %states_a.1 = (bf16[2048,1024]{1,0:T(8,128)(2,1)}, bf16[2048,1024]{1,0:T(8,128)(2,1)}, bf16[144,1024]{1,0:T(8,128)(2,1)}, bf16[2048,256]{1,0:T(8,128)(2,1)}) custom-call(bf16[2048,2048]{1,0:T(8,128)(2,1)} %feat.3, bf16[2048,128]{1,0:T(8,128)(2,1)} %get-tuple-element.21.lte, bf16[2048,128]{1,0:T(8,128)(2,1)} %get-tuple-element.22.le, f32[4,2048]{1,0:T(4,128)} %taps.3, ...), custom_call_target="tpu_custom_call" | custom-call | flops 1073741824 | bytes 12582912 | tf_op jit(solution)/shard_map/states_a/pallas_call | solution.py:372
  29.9 18.8 %states_b.1 = (bf16[2048,1024]{1,0:T(8,128)(2,1)}, bf16[2048,1024]{1,0:T(8,128)(2,1)}, bf16[144,1024]{1,0:T(8,128)(2,1)}, bf16[3,144,1024]{2,1,0:T(8,128)(2,1)}) custom-call(bf16[2048,2048]{1,0:T(8,128)(2,1)} %feat.3, bf16[2048,128]{1,0:T(8,128)(2,1)} %get-tuple-element.21.lte, bf16[2048,128]{1,0:T(8,128)(2,1)} %get-tuple-element.22.le, f32[4,2048]{1,0:T(4,128)} %taps.3, ...), custom_call_target="tpu_custom_call" | custom-call | flops 1073741824 | bytes 12582912 | tf_op jit(solution)/shard_map/states_b/pallas_call | solution.py:384
  48.8 19.0 %inside.1 = (bf16[2048,2048]{1,0:T(8,128)(2,1)}, bf16[3,144,1024]{2,1,0:T(8,128)(2,1)}) custom-call(bf16[2048,1024]{1,0:T(8,128)(2,1)} %get-tuple-element.26.x_a, bf16[2048,1024]{1,0:T(8,128)(2,1)} %get-tuple-element.27.x_b, bf16[2048,256]{1,0:T(8,128)(2,1)} %get-tuple-element.23.cb, f32[32,2048]{1,0:T(8,128)} %get-tuple-element.28.m, ...), custom_call_target="tpu_custom_call" | custom-call | flops 4294967296 | bytes 16777216 | tf_op jit(solution)/shard_map/inside/pallas_call | solution.py:395
  67.8 23.8 %carried.1 = (bf16[2048,2048]{1,0:T(8,128)(2,1)}, f32[16,128]{1,0:T(8,128)}) custom-call(s32[1]{0:T(128)} %bitcast.place, bf16[3,144,1024]{2,1,0:T(8,128)(2,1)} %get-tuple-element.25.recv_a, bf16[3,144,1024]{2,1,0:T(8,128)(2,1)} %get-tuple-element.31.recv_b, bf16[2048,1024]{1,0:T(8,128)(2,1)} %get-tuple-element.32.d_a, ...), custom_call_target="tpu_custom_call" | custom-call | flops 2147483648 | bytes 33554432 | tf_op jit(solution)/shard_map/carried/pallas_call | solution.py:406
  91.6 7.6 %sums.1.ss = f32[16,128]{1,0:T(8,128)} custom-call(f32[16,128]{1,0:T(8,128)} %get-tuple-element.35.ss), custom_call_target="tpu_custom_call" | custom-call | tf_op jit(solution)/shard_map/sums/pallas_call | solution.py:421
  99.1 8.1 %normalise.1 = bf16[2048,2048]{1,0:T(8,128)(2,1)} custom-call(f32[16,128]{1,0:T(8,128)} %sums.1.ss, bf16[2048,2048]{1,0:T(8,128)(2,1)} %get-tuple-element.36.g, f32[1,2048]{1,0:T(1,128)} %bitcast.7), custom_call_target="tpu_custom_call" | custom-call | flops 8388608 | bytes 16777216 | tf_op jit(solution)/shard_map/normalise/pallas_call | solution.py:433
  (1 shorter events, 0.0 us)
Async XLA Ops:
  1.5 9.6 %collective-permute-start = (bf16[3,2304]{1,0:T(4,128)(2,1)S(1)}, bf16[3,2304]{1,0:T(4,128)(2,1)S(1)}, u32[]{:S(2)}, u32[]{:S(2)}) collective-permute-start(bf16[3,2304]{1,0:T(4,128)(2,1)S(1)} %pad_maximum_fusion), channel_id=1, source_target_pairs={{0,8},{8,16},{16,24},{1,9},{9,17},{17,25},{2,10},{10,18},{18,26},{... | collective-permute-start | bytes 41480 | tf_op jit(solution)/shard_map/ppermute | solution.py:308

commit v3 on v2

--- a/solution.py
+++ b/solution.py
@@ -9,6 +9,7 @@
 INNER = 16384
 Q = 128
 ROWS = 512
+SHORT = 256
 STATE = 128
 HEAD = 64
 LOG2E = 1.4426950408889634
@@ -40,10 +41,8 @@
     return hi, mid, (v - hi) - mid
 
 
-def expander(heads, width, first_head):
-    row, col = iota((Q, width), 0), iota((Q, width), 1)
-    hit = ((row & (heads - 1)) == (col >> 6) + first_head) & (row < 4 * heads)
-    return jnp.where(hit, 1.0, 0.0).astype(BF)
+def over_channels(by_token, rs, h, first):
+    return jnp.where(first, by_token[rs, h : h + 1], by_token[rs, h + 1 : h + 2])
 
 
 def mix(tail, x, taps, bias):
@@ -54,29 +53,36 @@
     return silu(v).astype(BF)
 
 
-def prepare_kernel(raw, dlog, m_out, lt_out, le_out, lte_out):
+def prepare_kernel(raw, dlog, m_out, by_token, rows_out):
     heads, tokens = raw.shape
     blocks = tokens // Q
     r = jnp.concatenate([raw[:, c * Q : (c + 1) * Q] for c in range(blocks)], axis=0)
     step = jnp.maximum(r, 0.0) + jnp.log1p(jnp.exp(-jnp.abs(r)))
-    rate = jnp.broadcast_to(jnp.exp(dlog[...]) * -LOG2E, (heads, Q))
+    same = iota((heads, heads), 0) == iota((heads, heads), 1)
+    dlog_col = jnp.sum(jnp.where(same, dlog[...], 0.0), axis=1, keepdims=True)
+    rate = jnp.broadcast_to(jnp.exp(dlog_col) * -LOG2E, (heads, Q))
     ld = jnp.concatenate([rate] * blocks, axis=0) * step
     upto = jnp.where(iota((Q, Q), 0) <= iota((Q, Q), 1), 1.0, 0.0)
     lc = dot(ld, upto, precision=HI)
     m = lc - jnp.log(step) * LOG2E
     to_end = jnp.exp2(lc[:, Q - 1 : Q] - m)
-    pieces = split3(jnp.exp2(lc))
-    lane = iota((Q, Q), 1)
+    decay = jnp.exp2(lc)
+    ends = []
     for c in range(blocks):
         sl, rs = slice(c * Q, (c + 1) * Q), slice(c * heads, (c + 1) * heads)
         m_out[:, sl] = m[rs]
-        parts = [to_end[rs], *(piece[rs] for piece in pieces)]
-        if 4 * heads < Q:
-            parts.append(jnp.zeros((Q - 4 * heads, Q), F32))
-        t1 = jnp.transpose(jnp.concatenate(parts, axis=0))
-        lte_out[sl] = jnp.where(lane < heads, t1, 0.0).astype(BF)
-        le_out[sl] = jnp.where(lane >= heads, t1, 0.0).astype(BF)
-        lt_out[sl] = jnp.transpose(jnp.concatenate([lc[rs]] * (Q // heads), axis=0))
+        parts = [lc[rs], to_end[rs], decay[rs], jnp.zeros((Q - 3 * heads, Q), F32)]
+        turned = jnp.transpose(jnp.concatenate(parts, axis=0))
+        by_token[sl] = turned
+        ends.append(turned[Q - 1 : Q])
+    ends = jnp.concatenate(ends, axis=0)
+    lane = iota(ends.shape, 1)
+    ends = jnp.where((lane >= 2 * heads) & (lane < 3 * heads), ends, 0.0)
+    width = rows_out.shape[1]
+    row, col = iota((Q, width), 0), iota((Q, width), 1)
+    spread = jnp.where(row == (col >> 6) + 2 * heads, 1.0, 0.0).astype(BF)
+    hi, mid, lo = (piece.astype(BF) for piece in split3(ends))
+    rows_out[...] = dot(hi, spread) + dot(mid, spread) + dot(lo, spread)
 
 
 def exchange(n, src, dst, send_sem, recv_sem):
@@ -117,25 +123,23 @@
     return pl.ds(pl.multiple_of(i * Q, Q), Q)
 
 
-def states_body(first_head, heads, feat, lte, le, taps, off, ftail, input_map, x_out, d_out, e_out, ex, ftl, acc, dec):
+def states_body(first_head, heads, feat, by_token, decay, taps, off, ftail, input_map, x_out, d_out, e_out, ftl, acc, dec):
     c = pl.program_id(0)
     width = feat.shape[1]
 
     @pl.when(c == 0)
     def _():
-        ex[...] = expander(heads, width, first_head)
         ftl[...] = ftail[...]
         acc[...] = jnp.zeros_like(acc)
         dec[...] = jnp.ones_like(dec)
 
     def one(i, carry):
         rs = rows_of(i)
+        first = iota((Q, 128), 1) < HEAD
+        row = decay[pl.ds(c * chunks(feat) + i, 1), :]
         bt = jnp.transpose(input_map(rs).astype(F32)).astype(BF)
-        ends = le[pl.ds(pl.multiple_of(i * Q + Q - 16, 16), 16), :]
-        spread = jnp.concatenate([lte[rs, :], ends], axis=0)
         for j in range(width // 256):
             sl = slice(j * 256, (j + 1) * 256)
-            e = dot(spread, ex[:, sl])
             xw = []
             for k in range(2):
                 at = slice(j * 256 + k * 128, j * 256 + (k + 1) * 128)
@@ -143,12 +147,12 @@
                 f = mix(ftl[:, at], x, taps[:, at], off[:, at])
                 x_out[rs, at] = f
                 ftl[:, at] = x[Q - 8 :]
-                xw.append((f.astype(F32) * e[:Q, k * 128 : (k + 1) * 128]).astype(BF))
+                e = over_channels(by_token, rs, heads + first_head + 2 * (2 * j + k), first)
+                xw.append((f.astype(F32) * e).astype(BF))
             d = dot(bt, jnp.concatenate(xw, axis=1))
-            row = e[Q + 15 : Q + 16]
             d_out[rs, sl] = d.astype(BF)
-            acc[:, sl] = acc[:, sl] * row + d
-            dec[:, sl] = dec[:, sl] * row
+            acc[:, sl] = acc[:, sl] * row[:, sl] + d
+        dec[...] = dec[...] * row
         return carry
 
     lax.fori_loop(0, chunks(feat), one, 0)
@@ -163,7 +167,7 @@
 
 
 def states_a_kernel(
-    heads, feat, lte, le, taps, off, ftail, coup, tapc, offc, ctail, x_out, d_out, e_out, cb_out, ex, ftl, acc, dec, ctl
+    heads, feat, by_token, decay, taps, off, ftail, coup, tapc, offc, ctail, x_out, d_out, e_out, cb_out, ftl, acc, dec, ctl
 ):
     @pl.when(pl.program_id(0) == 0)
     def _():
@@ -178,16 +182,16 @@
             ctl[:, sl] = x[Q - 8 :]
         return f
 
-    states_body(0, heads, feat, lte, le, taps, off, ftail, input_map, x_out, d_out, e_out, ex, ftl, acc, dec)
+    states_body(0, heads, feat, by_token, decay, taps, off, ftail, input_map, x_out, d_out, e_out, ftl, acc, dec)
 
 
 def states_b_kernel(
-    heads, n, feat, lte, le, taps, off, ftail, cb, e_a, x_out, d_out, e_out, recv, ex, ftl, acc, dec, send_sem, recv_sem
+    heads, n, feat, by_token, decay, taps, off, ftail, cb, e_a, x_out, d_out, e_out, recv, ftl, acc, dec, send_sem, recv_sem
 ):
     finish = exchange(n, e_a, recv, send_sem, recv_sem)
     states_body(
-        heads // 2, heads, feat, lte, le, taps, off, ftail, lambda rs: cb[rs, :STATE],
-        x_out, d_out, e_out, ex, ftl, acc, dec,
+        heads // 2, heads, feat, by_token, decay, taps, off, ftail, lambda rs: cb[rs, :STATE],
+        x_out, d_out, e_out, ftl, acc, dec,
     )
     finish()
 
@@ -218,20 +222,35 @@
     finish()
 
 
-def carried_kernel(heads, others, place, recv_a, recv_b, d_a, d_b, le, cb, y_in, gate, g_out, ss_out, state, ex):
+def carried_kernel(
+    heads, others, n, recv_a, recv_b, d_a, d_b, by_token, decay, cb, y_in, gate,
+    g_out, ss_out, state, ss, slots, send_sem, recv_sem,
+):
     width = gate.shape[1]
     half = width // 2
     c = pl.program_id(0)
+    section, me = lax.axis_index("seq"), lax.axis_index("mp")
+
+    def copy(d):
+        return pltpu.make_async_remote_copy(
+            src_ref=ss, dst_ref=slots.at[d - 1], send_sem=send_sem.at[d - 1], recv_sem=recv_sem.at[d - 1],
+            device_id={"mp": lax.rem(me + d, n)}, device_id_type=pl.DeviceIdType.MESH,
+        )
 
     @pl.when(c == 0)
     def _():
-        ex[...] = expander(heads, width, 0)
+        barrier = pltpu.get_barrier_semaphore()
+        for d in range(1, n):
+            pl.semaphore_signal(
+                barrier, inc=1, device_id={"mp": lax.rem(me + d, n)}, device_id_type=pl.DeviceIdType.MESH
+            )
+        pl.semaphore_wait(barrier, n - 1)
         for j in range(width // 256):
             recv, at = (recv_a, j * 256) if j * 256 < half else (recv_b, j * 256 - half)
             total = jnp.zeros((STATE, 256), F32)
             through = jnp.ones((1, 256), F32)
             for d in range(others):
-                came = place[0] > d
+                came = section > d
                 end = recv[d, :STATE, at : at + 256].astype(F32)
                 rows = recv[d, STATE : STATE + 16, at : at + 256].astype(F32)
                 total = total + jnp.where(came, through * end, 0.0)
@@ -240,51 +259,38 @@
 
     def one(i, carry):
         rs = rows_of(i)
+        first = iota((Q, 128), 1) < HEAD
         out_map = cb[rs, STATE:]
-        lev = le[rs, :]
+        row = decay[pl.ds(c * chunks(gate) + i, 1), :]
         acc = jnp.zeros((Q, 128), F32)
         for j in range(width // 256):
             sl = slice(j * 256, (j + 1) * 256)
             d, at = (d_a, j * 256) if j * 256 < half else (d_b, j * 256 - half)
             s = state[:, sl]
-            e = dot(lev, ex[:, sl])
-            new = dot(out_map, s.astype(BF)) * e
-            state[:, sl] = s * e[Q - 1 : Q] + d[rs, at : at + 256].astype(F32)
+            new = dot(out_map, s.astype(BF))
+            state[:, sl] = s * row[:, sl] + d[rs, at : at + 256].astype(F32)
             for k in range(2):
                 part = slice(j * 256 + k * 128, j * 256 + (k + 1) * 128)
-                y = y_in[rs, part].astype(F32) + new[:, k * 128 : (k + 1) * 128]
+                e = over_channels(by_token, rs, 2 * heads + 2 * (2 * j + k), first)
+                y = y_in[rs, part].astype(F32) + new[:, k * 128 : (k + 1) * 128] * e
                 g = y * silu(gate[rs, part].astype(F32))
                 acc = acc + g * g
                 g_out[rs, part] = g.astype(BF)
-        ss = dot_rows(jnp.ones((8, Q), F32), acc, precision=HI)
-        ss_out[pl.ds(c * chunks(gate) + i, 1), :] = ss[0:1]
+        squares = dot_rows(jnp.ones((8, Q), F32), acc, precision=HI)
+        ss[pl.ds(c * chunks(gate) + i, 1), :] = squares[0:1]
         return carry
 
     lax.fori_loop(0, chunks(gate), one, 0)
 
-
-def sums_kernel(n, ss, out, slots, send_sem, recv_sem):
-    me = lax.axis_index("mp")
-
-    def copy(d):
-        return pltpu.make_async_remote_copy(
-            src_ref=ss, dst_ref=slots.at[d - 1], send_sem=send_sem.at[d - 1], recv_sem=recv_sem.at[d - 1],
-            device_id={"mp": lax.rem(me + d, n)}, device_id_type=pl.DeviceIdType.MESH,
-        )
-
-    barrier = pltpu.get_barrier_semaphore()
-    for d in range(1, n):
-        pl.semaphore_signal(
-            barrier, inc=1, device_id={"mp": lax.rem(me + d, n)}, device_id_type=pl.DeviceIdType.MESH
-        )
-    pl.semaphore_wait(barrier, n - 1)
-    for d in range(1, n):
-        copy(d).start()
-    total = ss[...]
-    for d in range(1, n):
-        copy(d).wait()
-        total = total + slots[d - 1]
-    out[...] = total
+    @pl.when(c == pl.num_programs(0) - 1)
+    def _():
+        for d in range(1, n):
+            copy(d).start()
+        total = ss[...]
+        for d in range(1, n):
+            copy(d).wait()
+            total = total + slots[d - 1]
+        ss_out[...] = total
 
 
 def norm_kernel(ss, g, gain, out):
@@ -333,6 +339,9 @@
     def rows(n, at=0):
         return pl.BlockSpec((ROWS, n), lambda c: (c, at))
 
+    def short(n):
+        return pl.BlockSpec((SHORT, n), lambda c: (c, 0))
+
     def side(n, at):
         return pl.BlockSpec((n, half), lambda c: (0, at))
 
@@ -344,31 +353,29 @@
     def cost(flops, moved):
         return pl.CostEstimate(flops=flops, bytes_accessed=moved * tokens * width, transcendentals=0)
 
-    m, lt, le, lte = pl.pallas_call(
+    m, by_token, decay = pl.pallas_call(
         prepare_kernel,
         in_specs=[vmem, vmem],
-        out_specs=[vmem] * 4,
-        out_shape=[
-            sds((heads, tokens), F32), sds((tokens, Q), F32), sds((tokens, Q), BF), sds((tokens, Q), BF),
-        ],
+        out_specs=[vmem] * 3,
+        out_shape=[sds((heads, tokens), F32), sds((tokens, Q), F32), sds((blocks, width), F32)],
         compiler_params=params(),
         cost_estimate=pl.CostEstimate(flops=work // 64, bytes_accessed=tokens * 1024, transcendentals=0),
         name="prepare",
-    )(step_raw, decay_log[:, None])
+    )(step_raw, decay_log[None])
 
     part = sds((tokens, half), BF)
     end_shape = sds((STATE + 16, half), BF)
     recv_shape = sds((seq - 1, STATE + 16, half), BF)
     keep = [
-        pltpu.VMEM((Q, half), BF), pltpu.VMEM((8, half), F32),
+        pltpu.VMEM((8, half), F32),
         pltpu.VMEM((STATE, half), F32), pltpu.VMEM((8, half), F32),
     ]
     sems = [pltpu.SemaphoreType.DMA((seq - 1,)), pltpu.SemaphoreType.DMA((seq - 1,))]
 
     def state_specs(at):
-        return [rows(half, at), rows(Q), rows(Q), side(4, at), side(1, at), side(8, at)]
-
-    state_args = (features, lte, le, feature_taps, feature_offset[None], prior)
+        return [rows(half, at), rows(Q), side(blocks, at), side(4, at), side(1, at), side(8, at)]
+
+    state_args = (features, by_token, decay, feature_taps, feature_offset[None], prior)
     x_a, d_a, e_a, cb = pl.pallas_call(
         functools.partial(states_a_kernel, heads),
         grid=grid,
@@ -402,39 +409,29 @@
         compiler_params=params(collective_id=1, has_side_effects=True),
         cost_estimate=cost(4 * work, 4),
         name="inside",
-    )(x_a, x_b, cb, m, lt, e_b)
-    g, ss = pl.pallas_call(
-        functools.partial(carried_kernel, heads, seq - 1),
-        grid=grid,
+    )(x_a, x_b, cb, m, by_token, e_b)
+    g, squares = pl.pallas_call(
+        functools.partial(carried_kernel, heads, seq - 1, mp),
+        grid=(tokens // SHORT,),
         in_specs=[
-            pl.BlockSpec(memory_space=pltpu.SMEM),
             whole(seq - 1, STATE + 16, half), whole(seq - 1, STATE + 16, half),
-            rows(half), rows(half), rows(Q), rows(2 * STATE), rows(width), rows(width),
+            short(half), short(half), short(Q), whole(blocks, width), short(2 * STATE), short(width), short(width),
         ],
-        out_specs=[rows(width), whole(blocks, Q)],
+        out_specs=[short(width), whole(blocks, Q)],
         out_shape=[sds((tokens, width), BF), sds((blocks, Q), F32)],
-        scratch_shapes=[pltpu.VMEM((STATE, width), F32), pltpu.VMEM((Q, width), BF)],
-        compiler_params=params(),
-        cost_estimate=cost(2 * work, 8),
-        name="carried",
-    )(lax.axis_index("seq").reshape(1), recv_a, recv_b, d_a, d_b, le, cb, y, gate_values)
-    squares = pl.pallas_call(
-        functools.partial(sums_kernel, mp),
-        in_specs=[vmem],
-        out_specs=vmem,
-        out_shape=sds((blocks, Q), F32),
         scratch_shapes=[
-            pltpu.VMEM((mp - 1, blocks, Q), F32),
+            pltpu.VMEM((STATE, width), F32), pltpu.VMEM((blocks, Q), F32), pltpu.VMEM((mp - 1, blocks, Q), F32),
             pltpu.SemaphoreType.DMA((mp - 1,)), pltpu.SemaphoreType.DMA((mp - 1,)),
         ],
         compiler_params=params(collective_id=2, has_side_effects=True),
-        name="sums",
-    )(ss)
+        cost_estimate=cost(2 * work, 8),
+        name="carried",
+    )(recv_a, recv_b, d_a, d_b, by_token, decay, cb, y, gate_values)
     return pl.pallas_call(
         norm_kernel,
-        grid=grid,
-        in_specs=[whole(blocks, Q), rows(width), whole(1, width)],
-        out_specs=rows(width),
+        grid=(tokens // SHORT,),
+        in_specs=[whole(blocks, Q), short(width), whole(1, width)],
+        out_specs=short(width),
         out_shape=sds((tokens, width), BF),
         compiler_params=params(),
         cost_estimate=cost(2 * tokens * width, 4),

time: 108 us -> 102 us (0.944)
  Pallas kernels: 98.8 us -> 94.3 us
  local copies, waits for them, and re-layouts: 2.81 us -> 1.46 us
    pallas_call x1, Pallas kernels: 18.2 us -> 15.4 us  [on_device(): pl.pallas_call(functools.partial(states_a_kernel, heads), grid=grid, in_s...]
    pallas_call x1, Pallas kernels: 18.8 us -> 17.1 us  [on_device(): pl.pallas_call(functools.partial(states_b_kernel, heads, seq), grid=grid,...]
    pallas_call x1, Pallas kernels: 19 us -> 20.7 us  [on_device(): pl.pallas_call(functools.partial(inside_kernel, seq), grid=grid, in_specs...]
    pallas_call x3 -> x2, Pallas kernels: 39.4 us -> 38 us  [the longest x1 28.1 us: on_device(): pl.pallas_call(functools.partial(carried_kernel, heads, seq - 1, mp), gri...]
    broadcast_in_dim x1 -> x0, local copies, waits for them, and re-layouts: 1.34 us -> none  [on_device(): decay_log[:, None]]
  transfers between devices with their start and end apart: 1 -> 1, of which waited for: 0 -> 0; matrix products, arithmetic and copies ran while one was open for 1% -> 0% of each run, Pallas kernels for 3% -> 3%
where the time goes in v3:
time: 102 us; the launch traced here: 101 us
  Pallas kernels  94.3 us (92%)
  starting transfers between devices  4.84 us (5%)
  local copies, waits for them, and re-layouts  1.46 us (1%)
    pallas_call x1, Pallas kernels, on_device(): pl.pallas_call(functools.partial(carried_kernel, heads, seq - 1, mp), gri...  28.1 us
    pallas_call x1, Pallas kernels, on_device(): pl.pallas_call(functools.partial(inside_kernel, seq), grid=grid, in_specs...  20.7 us
    pallas_call x1, Pallas kernels, on_device(): pl.pallas_call(functools.partial(states_b_kernel, heads, seq), grid=grid,...  17.1 us
    pallas_call x1, Pallas kernels, on_device(): pl.pallas_call(functools.partial(states_a_kernel, heads), grid=grid, in_s...  15.4 us
    pallas_call x1, Pallas kernels, on_device(): pl.pallas_call(norm_kernel, grid=(tokens // SHORT,), in_specs=[whole(bloc...  9.89 us
    ppermute x1, starting transfers between devices, passed_along(): return lax.ppermute(block, 'seq', route)  4.84 us
    pallas_call x1, Pallas kernels, on_device(): pl.pallas_call(prepare_kernel, in_specs=[vmem, vmem], out_specs=[vmem] *...  3.14 us
  transfers between devices with their start and end apart: 1, of which 0 were waited for; matrix products, arithmetic and copies ran while one was open for 0% of the time, Pallas kernels for 3%

profile of v3, /device:TPU:0, one launch (start us, length us, event | category | flops | bytes accessed | tf_op | source)
XLA Modules:
  0.0 101.3 jit_solution(3616568165018930873)
XLA Ops:
  0.0 0.7 slice.7
  0.7 0.8 slice.6
  1.5 4.8 %collective-permute-start = (bf16[3,2304]{1,0:T(4,128)(2,1)S(1)}, bf16[3,2304]{1,0:T(4,128)(2,1)S(1)}, u32[]{:S(2)}, u32[]{:S(2)}) collective-permute-start(bf16[3,2304]{1,0:T(4,128)(2,1)S(1)} %pad_maximum_fusion), channel_id=1, source_target_pairs={{0,8},{8,16},{16,24},{1,9},{9,17},{17,25},{2,10},{10,18},{18,26},{... | collective-permute-start | bytes 41480 | tf_op jit(solution)/shard_map/ppermute | solution.py:314
  6.3 3.1 %prepare.1 = (f32[32,2048]{1,0:T(8,128)}, f32[2048,128]{1,0:T(8,128)}, f32[16,2048]{1,0:T(8,128)}) custom-call(f32[32,2048]{1,0:T(8,128)} %raw.1, f32[1,32]{1,0:T(1,128)} %bitcast.8), custom_call_target="tpu_custom_call" | custom-call | flops 16777216 | bytes 2097152 | tf_op jit(solution)/shard_map/prepare/pallas_call | solution.py:356
  9.5 0.0 collective-permute-done
  9.5 0.6 pad_convert_fusion.ftail.ctail
  10.1 15.4 %states_a.1 = (bf16[2048,1024]{1,0:T(8,128)(2,1)}, bf16[2048,1024]{1,0:T(8,128)(2,1)}, bf16[144,1024]{1,0:T(8,128)(2,1)}, bf16[2048,256]{1,0:T(8,128)(2,1)}) custom-call(bf16[2048,2048]{1,0:T(8,128)(2,1)} %feat.3, f32[2048,128]{1,0:T(8,128)} %get-tuple-element.20.by_token.lt, f32[16,2048]{1,0:T(8,128)} %get-tuple-element.21.decay, f32[4,2048]{1,0:T(4,128)} %taps.3, ...), custom_call_target="tpu_custom_call" | custom-call | flops 1073741824 | bytes 12582912 | tf_op jit(solution)/shard_map/states_a/pallas_call | solution.py:379
  25.5 17.1 %states_b.1 = (bf16[2048,1024]{1,0:T(8,128)(2,1)}, bf16[2048,1024]{1,0:T(8,128)(2,1)}, bf16[144,1024]{1,0:T(8,128)(2,1)}, bf16[3,144,1024]{2,1,0:T(8,128)(2,1)}) custom-call(bf16[2048,2048]{1,0:T(8,128)(2,1)} %feat.3, f32[2048,128]{1,0:T(8,128)} %get-tuple-element.20.by_token.lt, f32[16,2048]{1,0:T(8,128)} %get-tuple-element.21.decay, f32[4,2048]{1,0:T(4,128)} %taps.3, ...), custom_call_target="tpu_custom_call" | custom-call | flops 1073741824 | bytes 12582912 | tf_op jit(solution)/shard_map/states_b/pallas_call | solution.py:391
  42.6 20.7 %inside.1 = (bf16[2048,2048]{1,0:T(8,128)(2,1)}, bf16[3,144,1024]{2,1,0:T(8,128)(2,1)}) custom-call(bf16[2048,1024]{1,0:T(8,128)(2,1)} %get-tuple-element.25.x_a, bf16[2048,1024]{1,0:T(8,128)(2,1)} %get-tuple-element.26.x_b, bf16[2048,256]{1,0:T(8,128)(2,1)} %get-tuple-element.22.cb, f32[32,2048]{1,0:T(8,128)} %get-tuple-element.27.m, ...), custom_call_target="tpu_custom_call" | custom-call | flops 4294967296 | bytes 16777216 | tf_op jit(solution)/shard_map/inside/pallas_call | solution.py:402
  63.3 28.1 %carried.1 = (bf16[2048,2048]{1,0:T(8,128)(2,1)}, f32[16,128]{1,0:T(8,128)}) custom-call(bf16[3,144,1024]{2,1,0:T(8,128)(2,1)} %get-tuple-element.24.recv_a, bf16[3,144,1024]{2,1,0:T(8,128)(2,1)} %get-tuple-element.29.recv_b, bf16[2048,1024]{1,0:T(8,128)(2,1)} %get-tuple-element.30.d_a, bf16[2048,1024]{1,0:T(8,128)(2,1)} %get-tuple-element.31.d_b, ...), custom_call_target="tpu_custom_call" | custom-call | flops 2147483648 | bytes 33554432 | tf_op jit(solution)/shard_map/carried/pallas_call | solution.py:413
  91.4 9.9 %normalise.1 = bf16[2048,2048]{1,0:T(8,128)(2,1)} custom-call(f32[16,128]{1,0:T(8,128)} %get-tuple-element.33.ss, bf16[2048,2048]{1,0:T(8,128)(2,1)} %get-tuple-element.34.g, f32[1,2048]{1,0:T(1,128)} %bitcast.6), custom_call_target="tpu_custom_call" | custom-call | flops 8388608 | bytes 16777216 | tf_op jit(solution)/shard_map/normalise/pallas_call | solution.py:430
  (1 shorter events, 0.0 us)
Async XLA Ops:
  1.5 8.0 %collective-permute-start = (bf16[3,2304]{1,0:T(4,128)(2,1)S(1)}, bf16[3,2304]{1,0:T(4,128)(2,1)S(1)}, u32[]{:S(2)}, u32[]{:S(2)}) collective-permute-start(bf16[3,2304]{1,0:T(4,128)(2,1)S(1)} %pad_maximum_fusion), channel_id=1, source_target_pairs={{0,8},{8,16},{16,24},{1,9},{9,17},{17,25},{2,10},{10,18},{18,26},{... | collective-permute-start | bytes 41480 | tf_op jit(solution)/shard_map/ppermute | solution.py:314

commit v4 on v3

--- a/solution.py
+++ b/solution.py
@@ -9,7 +9,7 @@
 INNER = 16384
 Q = 128
 ROWS = 512
-SHORT = 256
+SHORT = 512
 STATE = 128
 HEAD = 64
 LOG2E = 1.4426950408889634

time: 102 us -> 101 us (level)
    pallas_call x1, Pallas kernels: 9.89 us -> 8.05 us  [on_device(): pl.pallas_call(norm_kernel, grid=(tokens // SHORT,), in_specs=[whole(bloc...]
where the time goes in v4:
time: 101 us; the launch traced here: 100 us
  Pallas kernels  93.3 us (92%)
  starting transfers between devices  4.84 us (5%)
  local copies, waits for them, and re-layouts  1.46 us (1%)
    pallas_call x1, Pallas kernels, on_device(): pl.pallas_call(functools.partial(carried_kernel, heads, seq - 1, mp), gri...  28.9 us
    pallas_call x1, Pallas kernels, on_device(): pl.pallas_call(functools.partial(inside_kernel, seq), grid=grid, in_specs...  20.7 us
    pallas_call x1, Pallas kernels, on_device(): pl.pallas_call(functools.partial(states_b_kernel, heads, seq), grid=grid,...  17.1 us
    pallas_call x1, Pallas kernels, on_device(): pl.pallas_call(functools.partial(states_a_kernel, heads), grid=grid, in_s...  15.4 us
    pallas_call x1, Pallas kernels, on_device(): pl.pallas_call(norm_kernel, grid=(tokens // SHORT,), in_specs=[whole(bloc...  8.05 us
    ppermute x1, starting transfers between devices, passed_along(): return lax.ppermute(block, 'seq', route)  4.84 us
    pallas_call x1, Pallas kernels, on_device(): pl.pallas_call(prepare_kernel, in_specs=[vmem, vmem], out_specs=[vmem] *...  3.14 us
  transfers between devices with their start and end apart: 1, of which 0 were waited for; matrix products, arithmetic and copies ran while one was open for 0% of the time, Pallas kernels for 3%

profile of v4, /device:TPU:0, one launch (start us, length us, event | category | flops | bytes accessed | tf_op | source)
XLA Modules:
  0.0 100.3 jit_solution(5473911370308430102)
XLA Ops:
  0.0 0.7 slice.7
  0.7 0.8 slice.6
  1.5 4.8 %collective-permute-start = (bf16[3,2304]{1,0:T(4,128)(2,1)S(1)}, bf16[3,2304]{1,0:T(4,128)(2,1)S(1)}, u32[]{:S(2)}, u32[]{:S(2)}) collective-permute-start(bf16[3,2304]{1,0:T(4,128)(2,1)S(1)} %pad_maximum_fusion), channel_id=1, source_target_pairs={{0,8},{8,16},{16,24},{1,9},{9,17},{17,25},{2,10},{10,18},{18,26},{... | collective-permute-start | bytes 41480 | tf_op jit(solution)/shard_map/ppermute | solution.py:314
  6.3 3.1 %prepare.1 = (f32[32,2048]{1,0:T(8,128)}, f32[2048,128]{1,0:T(8,128)}, f32[16,2048]{1,0:T(8,128)}) custom-call(f32[32,2048]{1,0:T(8,128)} %raw.1, f32[1,32]{1,0:T(1,128)} %bitcast.8), custom_call_target="tpu_custom_call" | custom-call | flops 16777216 | bytes 2097152 | tf_op jit(solution)/shard_map/prepare/pallas_call | solution.py:356
  9.5 0.0 collective-permute-done
  9.5 0.6 pad_convert_fusion.ftail.ctail
  10.1 15.4 %states_a.1 = (bf16[2048,1024]{1,0:T(8,128)(2,1)}, bf16[2048,1024]{1,0:T(8,128)(2,1)}, bf16[144,1024]{1,0:T(8,128)(2,1)}, bf16[2048,256]{1,0:T(8,128)(2,1)}) custom-call(bf16[2048,2048]{1,0:T(8,128)(2,1)} %feat.3, f32[2048,128]{1,0:T(8,128)} %get-tuple-element.20.by_token.lt, f32[16,2048]{1,0:T(8,128)} %get-tuple-element.21.decay, f32[4,2048]{1,0:T(4,128)} %taps.3, ...), custom_call_target="tpu_custom_call" | custom-call | flops 1073741824 | bytes 12582912 | tf_op jit(solution)/shard_map/states_a/pallas_call | solution.py:379
  25.5 17.1 %states_b.1 = (bf16[2048,1024]{1,0:T(8,128)(2,1)}, bf16[2048,1024]{1,0:T(8,128)(2,1)}, bf16[144,1024]{1,0:T(8,128)(2,1)}, bf16[3,144,1024]{2,1,0:T(8,128)(2,1)}) custom-call(bf16[2048,2048]{1,0:T(8,128)(2,1)} %feat.3, f32[2048,128]{1,0:T(8,128)} %get-tuple-element.20.by_token.lt, f32[16,2048]{1,0:T(8,128)} %get-tuple-element.21.decay, f32[4,2048]{1,0:T(4,128)} %taps.3, ...), custom_call_target="tpu_custom_call" | custom-call | flops 1073741824 | bytes 12582912 | tf_op jit(solution)/shard_map/states_b/pallas_call | solution.py:391
  42.6 20.7 %inside.1 = (bf16[2048,2048]{1,0:T(8,128)(2,1)}, bf16[3,144,1024]{2,1,0:T(8,128)(2,1)}) custom-call(bf16[2048,1024]{1,0:T(8,128)(2,1)} %get-tuple-element.25.x_a, bf16[2048,1024]{1,0:T(8,128)(2,1)} %get-tuple-element.26.x_b, bf16[2048,256]{1,0:T(8,128)(2,1)} %get-tuple-element.22.cb, f32[32,2048]{1,0:T(8,128)} %get-tuple-element.27.m, ...), custom_call_target="tpu_custom_call" | custom-call | flops 4294967296 | bytes 16777216 | tf_op jit(solution)/shard_map/inside/pallas_call | solution.py:402
  63.3 28.9 %carried.1 = (bf16[2048,2048]{1,0:T(8,128)(2,1)}, f32[16,128]{1,0:T(8,128)}) custom-call(bf16[3,144,1024]{2,1,0:T(8,128)(2,1)} %get-tuple-element.24.recv_a, bf16[3,144,1024]{2,1,0:T(8,128)(2,1)} %get-tuple-element.29.recv_b, bf16[2048,1024]{1,0:T(8,128)(2,1)} %get-tuple-element.30.d_a, bf16[2048,1024]{1,0:T(8,128)(2,1)} %get-tuple-element.31.d_b, ...), custom_call_target="tpu_custom_call" | custom-call | flops 2147483648 | bytes 33554432 | tf_op jit(solution)/shard_map/carried/pallas_call | solution.py:413
  92.3 8.1 %normalise.1 = bf16[2048,2048]{1,0:T(8,128)(2,1)} custom-call(f32[16,128]{1,0:T(8,128)} %get-tuple-element.33.ss, bf16[2048,2048]{1,0:T(8,128)(2,1)} %get-tuple-element.34.g, f32[1,2048]{1,0:T(1,128)} %bitcast.6), custom_call_target="tpu_custom_call" | custom-call | flops 8388608 | bytes 16777216 | tf_op jit(solution)/shard_map/normalise/pallas_call | solution.py:430
  (1 shorter events, 0.0 us)
Async XLA Ops:
  1.5 8.0 %collective-permute-start = (bf16[3,2304]{1,0:T(4,128)(2,1)S(1)}, bf16[3,2304]{1,0:T(4,128)(2,1)S(1)}, u32[]{:S(2)}, u32[]{:S(2)}) collective-permute-start(bf16[3,2304]{1,0:T(4,128)(2,1)S(1)} %pad_maximum_fusion), channel_id=1, source_target_pairs={{0,8},{8,16},{16,24},{1,9},{9,17},{17,25},{2,10},{10,18},{18,26},{... | collective-permute-start | bytes 41480 | tf_op jit(solution)/shard_map/ppermute | solution.py:314
